TPU v7x, 256 devices: a whole 4x4x8 slice. The times are simulated.
256 devices in a mesh: ctx: 32 (over z_lo, x, core), exp: 8 (over z_hi, y).
Axes of the slice: x: 4, y: 4, z: 8 (z_hi: 2, z_lo: 4; z = z_hi * 4 + z_lo), core: 2. Of those that a mesh axis runs over, the one named last changes fastest.
Arguments:
- residual_in: bfloat16 [2048, 4096], P('ctx', 'exp'), may hold values from -16 to 16
- queries: bfloat16 [2048, 4096], P('ctx', 'exp'), may hold values from -5 to 5
- context_key_cache: bfloat16 [32768, 1024], P('ctx', 'exp'), may hold values from -5 to 5
- context_value_cache: bfloat16 [32768, 1024], P('ctx', 'exp'), may hold values from -10 to 10
- query_pos: int32 [2048], P('ctx'), may hold values from 0 to 32767, as said below
- norm_gain: bfloat16 [4096], replicated, may hold values from 0.099609375 to 1.8984375
- w_gate: bfloat16 [8, 14336, 4096], P('exp', 'ctx'), may hold values from -0.09375 to 0.09375
- w_up: bfloat16 [8, 14336, 4096], P('exp', 'ctx'), may hold values from -0.09375 to 0.09375
- w_down: bfloat16 [8, 14336, 4096], P('exp', 'ctx'), may hold values from -0.046875 to 0.046875
- expert_ids: int32 [2048, 2], P('ctx'), may hold values from 0 to 7, as said below
- kept_choices: int32 [2048, 2], P('ctx'), may hold values from 0 to 1, as said below
- gate_weights: float32 [2048, 2], P('ctx'), may hold values from 0.1 to 0.9
Outputs:
- layer_out: bfloat16 [2048, 4096], P('ctx', 'exp')
Inputs may be any that keep to these rules, and one draw needn't show every extreme that they name: `query_pos`: query token i stands at a context position from i * 16 to (i + 1) * 16 - 1. `expert_ids`: each row names 2 different experts. `kept_choices`: within each block of 64 consecutive tokens, the choices of an expert are ranked first choices before second choices and then by token, and exactly those of rank under 12 are kept; some expert keeps 12 choices from every block.
All inputs are finite; a program needn't handle non-finite values.
Results may differ from a plain program's by a relative error of at most 0.015.
Values may be sent and summed in bfloat16 or wider, within the bound.
A program may use at most 128 MiB of HBM per device.

v0:
```python
import jax
import jax.numpy as jnp
from jax import lax
from jax.sharding import PartitionSpec as P

HEAD_WIDTH = 128
TOP = 2


NEG_FILL = -1e30
NORM_EPS = 1e-05
FULL = lax.Precision.HIGHEST


def softmax_update(running, scores, visible, value_block):
    peaks, totals, accums = running
    masked = jnp.where(visible, scores, NEG_FILL)
    new_peaks = jnp.maximum(peaks, jnp.max(masked, axis=-1))
    weights = jnp.where(visible, jnp.exp(masked - new_peaks[..., None]), 0.0)
    new_totals = jnp.sum(weights, axis=-1)
    update = jnp.einsum(
        "rkgn,nkd->rkgd",
        weights.astype(jnp.bfloat16),
        value_block,
        preferred_element_type=jnp.float32,
    )
    return (new_peaks, new_totals, update)


def empty_state(count_of_rows, kv_heads, group_width):
    return (
        jnp.full((count_of_rows, kv_heads, group_width), NEG_FILL, jnp.float32),
        jnp.zeros((count_of_rows, kv_heads, group_width), jnp.float32),
        jnp.zeros((count_of_rows, kv_heads, group_width, HEAD_WIDTH), jnp.float32),
    )


def cycle_attention(queries, context_key_cache, context_value_cache, query_pos):
    count_of_rows = queries.shape[0]
    kv_heads = context_key_cache.shape[1] // HEAD_WIDTH
    group_width = queries.shape[1] // context_key_cache.shape[1]
    reshaped_array = queries.reshape(count_of_rows, kv_heads, group_width, HEAD_WIDTH)
    score_scale = HEAD_WIDTH ** (-0.5)
    key_piece = lax.all_gather(context_key_cache, "ctx", axis=0, tiled=True)
    value_piece = lax.all_gather(context_value_cache, "ctx", axis=0, tiled=True)
    length = key_piece.shape[0]
    scores = (
        jnp.einsum(
            "rkgd,nkd->rkgn",
            reshaped_array,
            key_piece.reshape(length, kv_heads, HEAD_WIDTH),
            preferred_element_type=jnp.float32,
        )
        * score_scale
    )
    positions = jnp.arange(length, dtype=jnp.int32)
    visible = (positions[None, :] <= query_pos[:, None])[:, None, None, :]
    peaks, totals, accums = softmax_update(
        empty_state(count_of_rows, kv_heads, group_width),
        scores,
        visible,
        value_piece.reshape(length, kv_heads, HEAD_WIDTH),
    )
    return (accums / totals[..., None]).reshape(count_of_rows, queries.shape[1])


def body(
    residual_in,
    queries,
    context_key_cache,
    context_value_cache,
    query_pos,
    norm_gain,
    w_gate,
    w_up,
    w_down,
    expert_ids,
    kept_choices,
    gate_weights,
):
    attended = cycle_attention(queries, context_key_cache, context_value_cache, query_pos)
    hidden = (residual_in.astype(jnp.float32) + attended).astype(jnp.bfloat16)
    full_rows = lax.all_gather(hidden, "exp", axis=1, tiled=True)
    widened = full_rows.astype(jnp.float32)
    normed = (
        widened
        * lax.rsqrt(jnp.mean(widened * widened, axis=-1, keepdims=True) + NORM_EPS)
        * norm_gain.astype(jnp.float32)
    ).astype(jnp.bfloat16)
    count_of_rows = residual_in.shape[0]
    expert_count = lax.axis_size("exp")
    slot_count = min(count_of_rows, max(2, count_of_rows * TOP * 3 // (4 * expert_count)))
    expert = lax.axis_index("exp")
    matched = ((expert_ids == expert) & (kept_choices == 1)).astype(jnp.int32)
    ordered = matched.T.reshape(TOP * count_of_rows)
    ranked = jnp.cumsum(ordered) - ordered
    slot_index = jnp.arange(slot_count, dtype=jnp.int32)
    picks = ((ordered[None, :] == 1) & (ranked[None, :] == slot_index[:, None])).astype(jnp.float32)
    slot_gate = jnp.dot(picks, gate_weights.T.reshape(TOP * count_of_rows), precision=FULL)
    token_pick = jnp.sum(picks.reshape(slot_count, TOP, count_of_rows), axis=1)
    selected = jnp.dot(
        token_pick.astype(jnp.bfloat16), normed, preferred_element_type=jnp.float32
    ).astype(jnp.bfloat16)
    gate_local = w_gate[0]
    up_local = w_up[0]
    down_local = w_down[0]
    contract = (((1,), (1,)), ((), ()))
    row_piece = lax.all_gather(selected, "ctx", axis=0, tiled=True)
    gate_part = lax.dot_general(row_piece, gate_local, contract, preferred_element_type=jnp.float32)
    up_part = lax.dot_general(row_piece, up_local, contract, preferred_element_type=jnp.float32)
    activated = (jax.nn.silu(gate_part) * up_part).astype(jnp.bfloat16)
    summed = lax.psum_scatter(
        jnp.dot(activated, down_local, preferred_element_type=jnp.float32).astype(jnp.bfloat16),
        "ctx",
        scatter_dimension=0,
        tiled=True,
    ).astype(jnp.float32)
    weighted = summed * slot_gate[:, None]
    returned = jnp.dot(token_pick.T, weighted, precision=FULL)
    mixed = lax.psum_scatter(
        returned.astype(jnp.bfloat16), "exp", scatter_dimension=1, tiled=True
    ).astype(jnp.float32)
    return (hidden.astype(jnp.float32) + mixed).astype(jnp.bfloat16)


def solution(mesh):
    in_specs = (
        P("ctx", "exp"),
        P("ctx", "exp"),
        P("ctx", "exp"),
        P("ctx", "exp"),
        P("ctx"),
        P(),
        P("exp", "ctx", None),
        P("exp", "ctx", None),
        P("exp", "ctx", None),
        P("ctx", None),
        P("ctx", None),
        P("ctx", None),
    )
    out_specs = P("ctx", "exp")
    return jax.shard_map(body, mesh=mesh, in_specs=in_specs, out_specs=out_specs, check_vma=False)
```

profile of v0, /device:TPU:2, one launch (start us, length us, event | category | flops | bytes accessed | tf_op | source)
XLA Modules:
  0.0 497.5 jit_solution(3608748591131427348)
XLA Ops:
  6.5 0.0 copy-start
  6.5 0.0 all-gather.5.cloned.1.call-start
  6.5 0.7 all-gather.5.cloned.1.call-update
  7.3 0.0 all-gather.7.cloned.1.call-start
  7.3 0.7 all-gather.7.cloned.1.call-update
  8.0 0.0 all-gather.9.cloned.1.call-start
  8.1 0.7 broadcast_compare_fusion
  8.8 0.1 broadcast_in_dim_reshape.5
  8.8 0.3 reduce-window_clone.1
  9.2 0.5 broadcast.55
  9.7 0.7 reduce.5
  10.3 0.1 reshape.110
  10.4 0.7 convert_element_type.57
  11.2 1.9 iota_compare_fusion
  13.0 68.3 %all-gather.5.cloned.1.call-done = bf16[32768,128]{1,0:T(8,128)(2,1)} async-done(((bf16[1024,128]{1,0:T(8,128)(2,1)}), bf16[32768,128]{1,0:T(8,128)(2,1)}) %all-gather.5.cloned.1.call-update) | async-done | bytes 8388624 | tf_op jit(solution)/shard_map/all_gather | solution.py:44
  81.4 0.0 copy-done
  81.4 18.0 %fusion.67 = (f32[64,4]{0,1:T(4,128)S(1)}, f32[64,1,4,32768]{3,0,2,1:T(8,128)}) fusion(bf16[32768,128]{1,0:T(8,128)(2,1)} %all-gather.5.cloned.1.call-done, pred[64,32768]{1,0:T(8,128)(4,1)S(1)} %iota_compare_fusion, bf16[64,512]{1,0:T(8,128)(2,1)S(1)} %copy-done), kind=kOutput, calls=%fused_computation.63 | convolution fusion | flops 2172649216 | bytes 44106752 | tf_op jit(solution)/shard_map/rkgd,nkd->rkgn/dot_general | solution.py:48
  99.3 14.9 %fusion.3 = f32[64,4]{0,1:T(4,128)S(1)} fusion(f32[64,1,4,32768]{3,0,2,1:T(8,128)} %get-tuple-element.8, f32[64,4]{0,1:T(4,128)S(1)} %broadcast_maximum_fusion, pred[64,32768]{1,0:T(8,128)(4,1)S(1)} %iota_compare_fusion), kind=kLoop, calls=%fused_computation.4 | loop fusion | flops 25165568 | bytes 35653632 | tf_op jit(solution)/shard_map/reduce_sum | solution.py:20
  114.2 0.0 copy-start.2
  114.2 36.9 %all-gather.7.cloned.1.call-done = bf16[32768,128]{1,0:T(8,128)(2,1)} async-done(((bf16[1024,128]{1,0:T(8,128)(2,1)}), bf16[32768,128]{1,0:T(8,128)(2,1)}) %all-gather.7.cloned.1.call-update) | async-done | bytes 8388624 | tf_op jit(solution)/shard_map/all_gather | solution.py:45
  151.1 16.4 %fusion.35 = f32[64,1,4,128]{3,0,2,1:T(8,128)S(1)} fusion(bf16[32768,128]{1,0:T(8,128)(2,1)} %all-gather.7.cloned.1.call-done, f32[64,1,4,32768]{3,0,2,1:T(8,128)} %get-tuple-element.8, f32[64,4]{0,1:T(4,128)S(1)} %broadcast_maximum_fusion, pred[64,32768]{1,0:T(8,128)(4,1)S(1)} %iota_compare_fusion, f32[64,4]{0,1:T(4,128)S(1)} %fusion.3), kind=kOutput, calls=%fused_computation.30 | convolution fusion | flops 2172682240 | bytes 44173312 | tf_op jit(solution)/shard_map/rkgn,nkd->rkgd/dot_general | solution.py:21
  167.5 0.1 copy.19
  167.6 0.0 copy-done.2
  167.6 44.7 %all_gather.14 = bf16[64,4096]{1,0:T(8,128)(2,1)S(1)} all-gather(bf16[64,512]{1,0:T(8,128)(2,1)S(1)} %fusion.51), channel_id=1, replica_groups=mesh['ctx'=32,'exp'=8] {'exp'}, dimensions={1}, use_global_device_ids=true | all-gather | bytes 589824 | tf_op jit(solution)/shard_map/all_gather | solution.py:83
  212.3 0.2 fusion.40
  212.6 1.0 fusion.13
  213.5 0.0 all-gather.9.cloned.1.call-update
  213.5 0.2 reduce-scatter.4.cloned.1.call-start
  213.8 0.1 broadcast_in_dim_reshape.6
  213.9 61.4 %all-gather.9.cloned.1.call-done = bf16[32,12,4096]{2,1,0:T(8,128)(2,1)} async-done(((bf16[1,12,4096]{2,1,0:T(8,128)(2,1)}), bf16[32,12,4096]{2,1,0:T(8,128)(2,1)}) %all-gather.9.cloned.1.call-update) | async-done | bytes 3145744 | tf_op jit(solution)/shard_map/all_gather | solution.py:108
  275.3 4.0 reshape.114
  279.2 5.0 %fusion.17 = f32[384,448]{0,1:T(8,128)} fusion(bf16[384,4096]{1,0:T(8,128)(2,1)S(1)} %reshape.114, bf16[1,448,4096]{2,1,0:T(8,128)(2,1)} %param.18), kind=kOutput, calls=%fused_computation.21 | convolution fusion | flops 1409286144 | bytes 7503872 | tf_op jit(solution)/shard_map/dot_general | solution.py:109
  284.2 0.0 copy-start.4
  284.2 0.0 copy-start.3
  284.2 0.0 copy-start.1
  284.2 8.9 %convolution_convert_fusion = bf16[384,4096]{1,0:T(8,128)(2,1)} fusion(bf16[1,448,4096]{2,1,0:T(8,128)(2,1)} %param.20, bf16[384,4096]{1,0:T(8,128)(2,1)S(1)} %reshape.114, bf16[1,448,4096]{2,1,0:T(8,128)(2,1)} %param.19, f32[384,448]{0,1:T(8,128)} %fusion.17), kind=kOutput, calls=%fused_computation.14 | convolution fusion | flops 2821177344 | bytes 14319616 | tf_op jit(solution)/shard_map/dot_general | solution.py:113
  293.1 78.1 %fusion = bf16[16,4096]{1,0:T(8,128)(2,1)S(1)} fusion(bf16[384,4096]{1,0:T(8,128)(2,1)} %convolution_convert_fusion), kind=kCustom, calls=%all-reduce-scatter | all-reduce-scatter fusion | flops 2097153 | bytes 3277824
  371.2 1.9 collective-permute-start
  373.2 1.9 collective-permute-start.1
  375.1 1.3 collective-permute-start.7
  376.4 1.3 collective-permute-start.2
  377.7 1.3 collective-permute-start.3
  379.0 0.0 collective-permute-done.7
  379.0 2.1 collective-permute-start.4
  381.1 0.0 collective-permute-done
  381.1 15.1 %collective-permute-start.5 = (bf16[16,4096]{1,0:T(8,128)(2,1)S(1)}, bf16[16,4096]{1,0:T(8,128)(2,1)S(1)}, u32[]{:S(2)}, u32[]{:S(2)}) collective-permute-start(bf16[16,4096]{1,0:T(8,128)(2,1)S(1)} %fusion), channel_id=1, source_target_pairs={{0,48},{8,56},{16,64},{24,72},{32,80},{40,88},{48,96},{56,104},{64... | collective-permute-start | bytes 393224
  396.2 0.0 collective-permute-done.1
  396.2 1.3 collective-permute-start.6
  397.5 0.0 copy-done.4
  397.6 0.1 reshape.117
  397.6 0.0 copy-done.3
  397.6 0.6 dynamic-slice.4
  398.9 0.1 convolution_bitcast_fusion
  399.0 0.0 collective-permute-done.2
  399.0 0.0 collective-permute-done.3
  399.0 0.0 collective-permute-done.4
  399.0 0.4 collective-permute-done.5
  399.4 2.1 collective-permute-done.6
  401.5 2.4 concatenate
  403.9 1.8 convolution_convert_fusion.1
  405.7 0.0 reduce-scatter.4.cloned.1.call-update
  405.8 83.7 %reduce-scatter.4.cloned.1.call-done = bf16[64,512]{1,0:T(8,128)(2,1)} async-done(((bf16[64,4096]{1,0:T(8,128)(2,1)}), bf16[64,512]{1,0:T(8,128)(2,1)}) %reduce-scatter.4.cloned.1.call-update) | async-done | bytes 65552 | tf_op jit(solution)/shard_map/reduce_scatter | solution.py:120
  489.5 1.5 add_convert_fusion
  491.0 0.0 copy-done.1
  (8 shorter events, 0.1 us)
Async XLA Ops:
  6.5 74.8 %copy-start = (bf16[64,512]{1,0:T(8,128)(2,1)S(1)}, bf16[64,512]{1,0:T(8,128)(2,1)}, u32[]{:S(2)}) copy-start(bf16[64,512]{1,0:T(8,128)(2,1)} %param.13) | copy-start | bytes 196612
  6.5 74.8 %all-gather.5.cloned.1.call-start = ((), (), s32[]{:S(2)}) async-start(), calls=%async_computation.1 | async-start | bytes 8650752 | tf_op jit(solution)/shard_map/all_gather | solution.py:44
  7.3 143.9 %all-gather.7.cloned.1.call-start = ((), (), s32[]{:S(2)}) async-start(), calls=%async_computation.2 | async-start | bytes 8650752 | tf_op jit(solution)/shard_map/all_gather | solution.py:45
  8.0 267.2 %all-gather.9.cloned.1.call-start = ((), (), s32[]{:S(2)}) async-start(), calls=%async_computation.4 | async-start | bytes 4325376 | tf_op jit(solution)/shard_map/all_gather | solution.py:108
  114.2 53.4 %copy-start.2 = (bf16[64,512]{1,0:T(8,128)(2,1)S(1)}, bf16[64,512]{1,0:T(8,128)(2,1)}, u32[]{:S(2)}) copy-start(bf16[64,512]{1,0:T(8,128)(2,1)} %param.12) | copy-start | bytes 196612
  213.5 275.9 %reduce-scatter.4.cloned.1.call-start = ((), (), s32[]{:S(2)}) async-start(), calls=%async_computation.3 | async-start | bytes 589824 | tf_op jit(solution)/shard_map/reduce_scatter | solution.py:120
  284.2 113.3 %copy-start.4 = (f32[64,2]{0,1:T(2,128)S(1)}, f32[64,2]{0,1:T(2,128)}, u32[]{:S(2)}) copy-start(f32[64,2]{0,1:T(2,128)} %param.23) | copy-start | bytes 1540
  284.2 113.4 %copy-start.3 = (u32[256]{0:T(256)S(1)}, u32[256]{0:T(256)}, u32[]{:S(2)}) copy-start(u32[256]{0:T(256)} %constant.33) | copy-start | bytes 3076
  284.2 206.8 %copy-start.1 = (bf16[64,512]{1,0:T(8,128)(2,1)S(1)}, bf16[64,512]{1,0:T(8,128)(2,1)}, u32[]{:S(2)}) copy-start(bf16[64,512]{1,0:T(8,128)(2,1)} %param.13) | copy-start | bytes 196612
  371.2 9.9 %collective-permute-start = (bf16[16,4096]{1,0:T(8,128)(2,1)S(1)}, bf16[16,4096]{1,0:T(8,128)(2,1)S(1)}, u32[]{:S(2)}, u32[]{:S(2)}) collective-permute-start(bf16[16,4096]{1,0:T(8,128)(2,1)S(1)} %fusion), channel_id=1, source_target_pairs={{0,8},{8,16},{16,24},{24,32},{32,40},{40,48},{48,56},{56,64},{64,7... | collective-permute-start | bytes 393224
  373.2 23.1 %collective-permute-start.1 = (bf16[16,4096]{1,0:T(8,128)(2,1)S(1)}, bf16[16,4096]{1,0:T(8,128)(2,1)S(1)}, u32[]{:S(2)}, u32[]{:S(2)}) collective-permute-start(bf16[16,4096]{1,0:T(8,128)(2,1)S(1)} %fusion), channel_id=1, source_target_pairs={{0,16},{8,24},{16,32},{24,40},{32,48},{40,56},{48,64},{56,72},{64,... | collective-permute-start | bytes 393224
  375.1 3.9 collective-permute-start.7
  376.4 22.6 %collective-permute-start.2 = (bf16[16,4096]{1,0:T(8,128)(2,1)S(1)}, bf16[16,4096]{1,0:T(8,128)(2,1)S(1)}, u32[]{:S(2)}, u32[]{:S(2)}) collective-permute-start(bf16[16,4096]{1,0:T(8,128)(2,1)S(1)} %fusion), channel_id=1, source_target_pairs={{0,24},{8,32},{16,40},{24,48},{32,56},{40,64},{48,72},{56,80},{64,... | collective-permute-start | bytes 393224
  377.7 21.3 %collective-permute-start.3 = (bf16[16,4096]{1,0:T(8,128)(2,1)S(1)}, bf16[16,4096]{1,0:T(8,128)(2,1)S(1)}, u32[]{:S(2)}, u32[]{:S(2)}) collective-permute-start(bf16[16,4096]{1,0:T(8,128)(2,1)S(1)} %fusion), channel_id=1, source_target_pairs={{0,32},{8,40},{16,48},{24,56},{32,64},{40,72},{48,80},{56,88},{64,... | collective-permute-start | bytes 393224
  379.0 20.0 %collective-permute-start.4 = (bf16[16,4096]{1,0:T(8,128)(2,1)S(1)}, bf16[16,4096]{1,0:T(8,128)(2,1)S(1)}, u32[]{:S(2)}, u32[]{:S(2)}) collective-permute-start(bf16[16,4096]{1,0:T(8,128)(2,1)S(1)} %fusion), channel_id=1, source_target_pairs={{0,40},{8,48},{16,56},{24,64},{32,72},{40,80},{48,88},{56,96},{64,... | collective-permute-start | bytes 393224
  381.1 18.2 %collective-permute-start.5 = (bf16[16,4096]{1,0:T(8,128)(2,1)S(1)}, bf16[16,4096]{1,0:T(8,128)(2,1)S(1)}, u32[]{:S(2)}, u32[]{:S(2)}) collective-permute-start(bf16[16,4096]{1,0:T(8,128)(2,1)S(1)} %fusion), channel_id=1, source_target_pairs={{0,48},{8,56},{16,64},{24,72},{32,80},{40,88},{48,96},{56,104},{64... | collective-permute-start | bytes 393224
  396.2 5.3 %collective-permute-start.6 = (bf16[16,4096]{1,0:T(8,128)(2,1)S(1)}, bf16[16,4096]{1,0:T(8,128)(2,1)S(1)}, u32[]{:S(2)}, u32[]{:S(2)}) collective-permute-start(bf16[16,4096]{1,0:T(8,128)(2,1)S(1)} %fusion), channel_id=1, source_target_pairs={{0,56},{8,64},{16,72},{24,80},{32,88},{40,96},{48,104},{56,112},{6... | collective-permute-start | bytes 393224
Sparse Core Ops, SparseCore 0:
  9.2 72.0 all-gather.4
  83.2 67.8 all-gather.6
  213.7 61.5 all-gather.8
  405.9 83.5 reduce-scatter.3
where the time goes:
time: 498 us
  waiting for transfers between devices  254 us (51%)
  blocking collectives  123 us (25%)
  matrix products  51.1 us (10%)
  starting transfers between devices  26.5 us (5%)
  other arithmetic  20.9 us (4%)
  between operations  14 us (3%)
  local copies, waits for them, and re-layouts  7.95 us (2%)
    reduce_scatter x1, waiting for transfers between devices, body(): lax.psum_scatter(returned.astype(jnp.bfloat16), 'exp', scatter_dimension=...  83.7 us
    unnamed x1, blocking collectives  78.1 us
    all_gather x1, waiting for transfers between devices, cycle_attention(): key_piece = lax.all_gather(context_key_cache, 'ctx', axis=0, tiled=True)  68.3 us
    all_gather x1, waiting for transfers between devices, body(): row_piece = lax.all_gather(selected, 'ctx', axis=0, tiled=True)  61.4 us
    all_gather x1, blocking collectives, body(): full_rows = lax.all_gather(hidden, 'exp', axis=1, tiled=True)  44.7 us
    all_gather x1, waiting for transfers between devices, cycle_attention(): value_piece = lax.all_gather(context_value_cache, 'ctx', axis=0, tiled=True)  36.9 us
    unnamed x8, starting transfers between devices  26.2 us
    dot_general x1, matrix products, cycle_attention(): jnp.einsum('rkgd,nkd->rkgn', reshaped_array, key_piece.reshape(length, kv...  18 us
  transfers between devices with their start and end apart: 12, of which 6 were waited for; matrix products, arithmetic and copies ran while one was open for 8% of the time, Pallas kernels for 0%

commit v1 on v0

v1 whole, which is shorter than its diff:
```python
import math
import types

import jax
import jax.numpy as jnp
from jax import lax
from jax.experimental import pallas as pl
from jax.experimental.pallas import tpu as pltpu
from jax.sharding import PartitionSpec as P

BF = jnp.bfloat16
F32 = jnp.float32
MESH = pl.DeviceIdType.MESH
NT = (((1,), (1,)), ((), ()))
NN = (((1,), (0,)), ((), ()))
HEAD = 128
ROWS = 64
HEADS = 4
TALL = ROWS * HEADS
KEYS = 1024
MODEL = 4096
HIDDEN = 448
EXPERTS = 8
SLOTS = 12
PIECE = SLOTS * HEADS
WIDE = EXPERTS * HEAD
NEG = -1e30
EPS = 1e-05
SCALE = HEAD ** (-0.5) * math.log2(math.e)


class Place:
    def __init__(self):
        self.me = lax.axis_index("ctx")
        self.e = lax.axis_index("exp")
        self.z = lax.div(self.me, 8)
        self.x = lax.rem(lax.div(self.me, 2), 4)
        self.a = lax.rem(self.me, 2)
        z = self.z
        self.zk = [z, z + 1 - 2 * lax.rem(z, 2), z + 2 - 4 * lax.div(z, 2), 3 - z]
        self.xr = [self.x] + [lax.rem(self.x + r, 4) for r in (1, 2, 3)]
        self.sib = self.spot(self.z, self.x, 1 - self.a)
        self.right = self.spot(self.z, self.xr[1], self.a)
        self.left = self.spot(self.z, self.xr[3], self.a)
        self.ek = [lax.rem(self.e + j, EXPERTS) for j in range(EXPERTS)]

    def spot(self, z, x, a):
        return z * 8 + x * 2 + a

    def piece(self, k, r, a):
        return self.spot(self.zk[k], self.xr[r], a)

    def column(self, k):
        return self.spot(self.zk[k], self.x, self.a)


class Mail:
    def __init__(self, place, sems):
        self.place, self.sems, self.used, self.open = place, sems, 0, []

    def ship(self, src, dst, recv_sem, ctx=None, exp=None):
        target = {"ctx": ctx} if exp is None else {"exp": exp}
        copy = pltpu.make_async_remote_copy(
            src_ref=src,
            dst_ref=dst,
            send_sem=self.sems.at[self.used],
            recv_sem=recv_sem,
            device_id=target,
            device_id_type=MESH,
        )
        self.used += 1
        copy.start()
        self.open.append(copy)

    def drain(self):
        for copy in self.open:
            copy.wait_send()
        self.open = []


def landed(slot, recv_sem, place):
    pltpu.make_async_remote_copy(
        src_ref=slot,
        dst_ref=slot,
        send_sem=recv_sem,
        recv_sem=recv_sem,
        device_id={"ctx": place.sib},
        device_id_type=MESH,
    ).wait_recv()


def wide(x, times):
    return jnp.concatenate([x] * times, axis=1)


def greet(place, with_exp):
    barrier = pltpu.get_barrier_semaphore()
    peers = [{"ctx": c} for c in (place.sib, place.right, place.left)]
    peers += [{"ctx": place.column(k)} for k in (1, 2, 3)]
    if with_exp:
        peers += [{"exp": place.ek[j]} for j in range(1, EXPERTS)]
    for peer in peers:
        pl.semaphore_signal(barrier, inc=1, device_id=peer, device_id_type=MESH)
    pl.semaphore_wait(barrier, len(peers))


def attention(place, q_ref, k_ref, v_ref, pos_ref, s):
    z, a = place.z, place.a
    mail = Mail(place, s.kv_send)

    def q_copy(k):
        return pltpu.make_async_remote_copy(
            src_ref=q_ref,
            dst_ref=s.qg.at[z],
            send_sem=s.q_send.at[k],
            recv_sem=s.q_recv.at[z],
            device_id={"ctx": place.spot(z - k, place.x, a)},
            device_id_type=MESH,
        )

    for k in (1, 2, 3):

        @pl.when(z >= k)
        def _(k=k):
            q_copy(k).start()

    mine = place.x * 2 + a

    def unit(r, core):
        return place.xr[r] * 2 + core

    for target in (place.sib, place.right, place.left):
        mail.ship(k_ref, s.kg.at[mine], s.k_recv.at[mine], ctx=target)
    for target in (place.sib, place.right, place.left):
        mail.ship(v_ref, s.vg.at[mine], s.v_recv.at[mine], ctx=target)

    def got_k(r, core):
        u = unit(r, core)
        landed(s.kg.at[u], s.k_recv.at[u], place)
        return u

    def got_v(r, core):
        u = unit(r, core)
        landed(s.vg.at[u], s.v_recv.at[u], place)
        return u

    def pass_k(u, target):
        mail.ship(s.kg.at[u], s.kg.at[u], s.k_recv.at[u], ctx=target)

    def pass_v(u, target):
        mail.ship(s.vg.at[u], s.vg.at[u], s.v_recv.at[u], ctx=target)

    row = lax.broadcasted_iota(jnp.int32, (ROWS, ROWS), 0)
    col = lax.broadcasted_iota(jnp.int32, (ROWS, ROWS), 1)
    pos = pos_ref[...].astype(F32) - (place.me * KEYS).astype(F32)
    column = jnp.sum(jnp.where(row == col, pos, 0.0), axis=1, keepdims=True)
    pos_col = jnp.concatenate([column] * HEADS, axis=0)

    def prepare(zq, q):
        for h in range(HEADS):
            full = q[:, h * HEAD : (h + 1) * HEAD].astype(F32) * SCALE
            high = full.astype(BF)
            low = (full - high.astype(F32)).astype(BF)
            s.q2[zq, h * ROWS : (h + 1) * ROWS, :HEAD] = high
            s.q2[zq, h * ROWS : (h + 1) * ROWS, HEAD:] = low
        s.peak[zq] = jnp.full((TALL, HEAD), NEG, F32)
        s.acc[zq] = jnp.zeros((TALL, 2 * HEAD), F32)

    s.vv[:, HEAD:] = jnp.ones((KEYS, HEAD), BF)
    prepare(z, q_ref[...])

    def update(zq, masked):
        scores = lax.dot_general(s.q2[zq], s.kk[...], NT, preferred_element_type=F32)
        if masked:
            key = lax.broadcasted_iota(jnp.int32, (TALL, KEYS), 1).astype(F32)
            scores = jnp.where(key <= pos_col, scores, NEG)
        old = s.peak[zq]
        new = jnp.maximum(old, jnp.max(scores, axis=1, keepdims=True))
        probs = jnp.exp2(scores - wide(new, KEYS // HEAD)).astype(BF)
        part = jnp.dot(probs, s.vv[...], preferred_element_type=F32)
        shrink = jnp.exp2(old - new)
        s.acc[zq] = s.acc[zq] * wide(shrink, 2) + part
        s.peak[zq] = new

    def load(kr, vr):
        key = kr[...]
        s.kk[:, :HEAD] = key
        s.kk[:, HEAD:] = key
        s.vv[:, :HEAD] = vr[...]

    def others(_=None):
        def step(i, carry):
            update(z + 1 + i, False)
            return carry

        lax.fori_loop(0, 3 - z, step, 0)

    def whole(u):
        load(s.kg.at[u], s.vg.at[u])

        @pl.when(u < mine)
        def _():
            update(z, False)

        others()

    load(k_ref, v_ref)
    update(z, True)
    for k in (1, 2, 3):

        @pl.when(z + k <= 3)
        def _(k=k):
            landed(s.qg.at[z + k], s.q_recv.at[z + k], place)
            prepare(z + k, s.qg[z + k])

    others()
    u = got_k(0, 1 - a)
    got_v(0, 1 - a)
    whole(u)
    kl = got_k(3, a)
    pass_k(kl, place.right)
    pass_k(kl, place.sib)
    kr = got_k(1, a)
    pass_k(kr, place.sib)
    vr = got_v(1, a)
    pass_v(vr, place.left)
    pass_v(vr, place.sib)
    vl = got_v(3, a)
    pass_v(vl, place.sib)
    whole(kl)
    whole(kr)
    ko = got_k(2, a)
    pass_k(ko, place.sib)
    for r in (3, 1):
        u = got_k(r, 1 - a)
        got_v(r, 1 - a)
        whole(u)
    vo = got_v(2, a)
    pass_v(vo, place.sib)
    whole(ko)
    u = got_k(2, 1 - a)
    got_v(2, 1 - a)
    load(s.kg.at[u], s.vg.at[u])

    eye_r = lax.broadcasted_iota(jnp.int32, (HEAD, HEAD), 0)
    eye_c = lax.broadcasted_iota(jnp.int32, (HEAD, HEAD), 1)
    eye = eye_r == eye_c

    def back(zq):
        def part(src, dst, send, recv):
            return pltpu.make_async_remote_copy(
                src_ref=src.at[zq],
                dst_ref=dst.at[z],
                send_sem=send.at[zq],
                recv_sem=recv.at[z],
                device_id={"ctx": place.spot(zq, place.x, a)},
                device_id_type=MESH,
            )

        return (
            part(s.o_out, s.o_in, s.o_send, s.o_recv),
            part(s.l_out, s.l_in, s.l_send, s.l_recv),
        )

    def finish(i, carry):
        zq = 3 - i
        update(zq, False)
        total = s.acc[zq, :, HEAD:]
        s.o_out[zq] = (s.acc[zq, :, :HEAD] / total).astype(BF)
        level = s.peak[zq] + jnp.log2(total)
        for half in range(2):
            block = level[half * HEAD : (half + 1) * HEAD]
            s.l_out[zq, half : half + 1, :] = jnp.sum(
                jnp.where(eye, block, 0.0), axis=0, keepdims=True
            )
        for copy in back(zq):
            copy.start()
        return carry

    lax.fori_loop(0, 3 - z, finish, 0)

    @pl.when(u < mine)
    def _():
        update(z, False)

    for k in (1, 2, 3):

        @pl.when(z >= k)
        def _(k=k):
            zs = z - k
            landed(s.o_in.at[zs], s.o_recv.at[zs], place)
            landed(s.l_in.at[zs], s.l_recv.at[zs], place)
            spread = []
            for half in range(2):
                line = s.l_in[zs, half : half + 1, :]
                spread.append(jnp.sum(jnp.where(eye, line, 0.0), axis=1, keepdims=True))
            level = jnp.concatenate(spread, axis=0) + jnp.zeros((TALL, HEAD), F32)
            old = s.peak[z]
            new = jnp.maximum(old, level)
            shrink, weight = jnp.exp2(old - new), jnp.exp2(level - new)
            s.acc[z, :, :HEAD] = s.acc[z, :, :HEAD] * shrink + weight * s.o_in[zs].astype(F32)
            s.acc[z, :, HEAD:] = s.acc[z, :, HEAD:] * shrink + weight
            s.peak[z] = new

    for k in (1, 2, 3):

        @pl.when(z >= k)
        def _(k=k):
            q_copy(k).wait_send()

    def settle(i, carry):
        for copy in back(3 - i):
            copy.wait_send()
        return carry

    lax.fori_loop(0, 3 - z, settle, 0)
    mail.drain()
    return s.acc[z, :, :HEAD] / s.acc[z, :, HEAD:]


ATTEND_SCRATCH = dict(
    kg=pltpu.VMEM((8, KEYS, HEAD), BF),
    vg=pltpu.VMEM((8, KEYS, HEAD), BF),
    qg=pltpu.VMEM((4, ROWS, HEADS * HEAD), BF),
    q2=pltpu.VMEM((4, TALL, 2 * HEAD), BF),
    kk=pltpu.VMEM((KEYS, 2 * HEAD), BF),
    vv=pltpu.VMEM((KEYS, 2 * HEAD), BF),
    peak=pltpu.VMEM((4, TALL, HEAD), F32),
    acc=pltpu.VMEM((4, TALL, 2 * HEAD), F32),
    o_out=pltpu.VMEM((4, TALL, HEAD), BF),
    o_in=pltpu.VMEM((4, TALL, HEAD), BF),
    l_out=pltpu.VMEM((4, 8, HEAD), F32),
    l_in=pltpu.VMEM((4, 8, HEAD), F32),
    kv_send=pltpu.SemaphoreType.DMA((16,)),
    q_send=pltpu.SemaphoreType.DMA((4,)),
    q_recv=pltpu.SemaphoreType.DMA((4,)),
    k_recv=pltpu.SemaphoreType.DMA((8,)),
    v_recv=pltpu.SemaphoreType.DMA((8,)),
    o_send=pltpu.SemaphoreType.DMA((4,)),
    o_recv=pltpu.SemaphoreType.DMA((4,)),
    l_send=pltpu.SemaphoreType.DMA((4,)),
    l_recv=pltpu.SemaphoreType.DMA((4,)),
)


def attend_kernel(res_ref, q_ref, k_ref, v_ref, pos_ref, out_ref, *scratch):
    s = types.SimpleNamespace(**dict(zip(ATTEND_SCRATCH, scratch)))
    place = Place()
    greet(place, False)
    attended = attention(place, q_ref, k_ref, v_ref, pos_ref, s)
    for h in range(HEADS):
        res = res_ref[:, h * HEAD : (h + 1) * HEAD].astype(F32)
        out_ref[h * ROWS : (h + 1) * ROWS, :] = (res + attended[h * ROWS : (h + 1) * ROWS]).astype(BF)


def attend_call(residual_in, queries, keys, values, pos):
    vmem = pl.BlockSpec(memory_space=pltpu.VMEM)
    return pl.pallas_call(
        attend_kernel,
        out_shape=jax.ShapeDtypeStruct((TALL, HEAD), BF),
        in_specs=[vmem] * 5,
        out_specs=vmem,
        scratch_shapes=list(ATTEND_SCRATCH.values()),
        compiler_params=pltpu.CompilerParams(
            collective_id=0, has_side_effects=True, vmem_limit_bytes=40 * 2**20
        ),
        name="attend",
    )(residual_in, queries, keys, values, pos.reshape(1, ROWS))


def steps(index, edges):
    return sum((index >= edge).astype(jnp.int32) for edge in edges)


def slot_columns(ids_ref, kept_ref):
    lane = lax.broadcasted_iota(jnp.int32, (ROWS, HEAD), 1)
    flags = []
    for k in range(2):
        hit = (ids_ref[:, k : k + 1] == lane) & (kept_ref[:, k : k + 1] == 1)
        flags.append(hit.astype(F32))
    before = (
        lax.broadcasted_iota(jnp.int32, (ROWS, ROWS), 1)
        < lax.broadcasted_iota(jnp.int32, (ROWS, ROWS), 0)
    ).astype(F32)
    columns = []
    passed = jnp.zeros((1, HEAD), F32)
    for flag in flags:
        rank = passed + jnp.dot(before, flag, preferred_element_type=F32)
        passed = passed + jnp.sum(flag, axis=0, keepdims=True)
        slot = flag * (lane.astype(F32) * SLOTS + rank + 1.0)
        columns.append(jnp.sum(slot, axis=1, keepdims=True) - 1.0)
    return columns


def slot_and_head(index):
    expert = steps(index, range(PIECE, EXPERTS * PIECE, PIECE))
    within = index - expert * PIECE
    head = steps(within, range(SLOTS, PIECE, SLOTS))
    return (expert * SLOTS + within - head * SLOTS).astype(F32), head


def pick_rows(columns):
    shape = (EXPERTS * PIECE, TALL)
    slot, head = slot_and_head(lax.broadcasted_iota(jnp.int32, shape, 0))
    lane = lax.broadcasted_iota(jnp.int32, (ROWS, TALL), 1)
    group = steps(lane, range(ROWS, TALL, ROWS))
    same = lax.broadcasted_iota(jnp.int32, (ROWS, TALL), 0) == lane - group * ROWS
    hit = jnp.zeros(shape, F32)
    for column in columns:
        line = jnp.sum(jnp.where(same, column, 0.0), axis=0, keepdims=True)
        hit = hit + (line == slot).astype(F32)
    lanes = lax.broadcasted_iota(jnp.int32, shape, 1)
    hit = jnp.where(steps(lanes, range(ROWS, TALL, ROWS)) == head, hit, 0.0)
    return hit.astype(BF)


def place_rows(column):
    shape = (TALL, EXPERTS * PIECE)
    slot, head = slot_and_head(lax.broadcasted_iota(jnp.int32, shape, 1))
    tall = jnp.concatenate([column] * HEADS, axis=0)
    rows = lax.broadcasted_iota(jnp.int32, shape, 0)
    hit = (slot == tall) & (steps(rows, range(ROWS, TALL, ROWS)) == head)
    return hit.astype(F32).astype(BF)


def swap_matrix():
    side = 4 * PIECE
    row = lax.broadcasted_iota(jnp.int32, (side, side), 0)
    col = lax.broadcasted_iota(jnp.int32, (side, side), 1)
    first = steps(row, (PIECE, 2 * PIECE, 3 * PIECE))
    within = row - first * PIECE
    second = steps(within, (SLOTS, 2 * SLOTS, 3 * SLOTS))
    slot = within - second * SLOTS
    return (col == second * PIECE + first * SLOTS + slot).astype(F32).astype(BF)


def fetch_weights(gate_hbm, up_hbm, down_hbm, s):
    pairs = ((gate_hbm, s.w_gate), (up_hbm, s.w_up), (down_hbm, s.w_down))
    return [
        pltpu.make_async_copy(hbm.at[0], vmem, s.w_sem.at[i])
        for i, (hbm, vmem) in enumerate(pairs)
    ]


def experts(place, hidden, ids_ref, kept_ref, gate_ref, gain_ref, weights, s):
    a, e = place.a, place.e
    mail = Mail(place, s.send)

    columns = slot_columns(ids_ref, kept_ref)
    chosen = jnp.dot(pick_rows(columns), hidden, preferred_element_type=F32).astype(BF)
    for j in range(EXPERTS):
        s.pick[j] = chosen[j * PIECE : (j + 1) * PIECE]
    for j in range(1, EXPERTS):
        to = place.ek[j]
        mail.ship(s.pick.at[to], s.picked.at[e], s.picked_recv.at[e], exp=to)
    s.picked[e] = s.pick[e]
    swap = swap_matrix()
    ring = lax.broadcasted_iota(jnp.int32, (PIECE, PIECE), 0)
    ring = ring - SLOTS * steps(ring, (SLOTS, 2 * SLOTS, 3 * SLOTS))
    lap = lax.broadcasted_iota(jnp.int32, (PIECE, PIECE), 1)
    lap = lap - SLOTS * steps(lap, (SLOTS, 2 * SLOTS, 3 * SLOTS))
    alike = (ring == lap).astype(F32)
    place_of = [place_rows(column) for column in columns]
    for k in range(2):
        s.spread[k] = place_of[k]
    for j in range(1, EXPERTS):
        f = place.ek[j]
        landed(s.picked.at[f], s.picked_recv.at[f], place)

    squares = jnp.zeros((PIECE, HEAD), F32)
    for f in range(EXPERTS):
        x = s.picked[f].astype(F32)
        squares = squares + x * x
    squares = jnp.sum(squares, axis=1, keepdims=True) + jnp.zeros((PIECE, HEAD), F32)
    total = jnp.dot(alike, squares, precision=lax.Precision.HIGHEST, preferred_element_type=F32)
    scale = lax.rsqrt(total / MODEL + EPS)
    part = lax.broadcasted_iota(jnp.int32, (PIECE, HEAD), 0)
    part = steps(part, (SLOTS, 2 * SLOTS, 3 * SLOTS))
    me = place.me
    for f in range(EXPERTS):
        gain = gain_ref[f * HEADS : f * HEADS + 1, :]
        for h in range(1, HEADS):
            gain = jnp.where(part >= h, gain_ref[f * HEADS + h : f * HEADS + h + 1, :], gain)
        s.rows[me, :, f * HEAD : (f + 1) * HEAD] = (s.picked[f].astype(F32) * scale * gain).astype(BF)

    def forward(slot, *targets):
        for target in targets:
            mail.ship(s.rows.at[slot], s.rows.at[slot], s.rows_recv.at[slot], ctx=target)

    def got(k, r, core):
        slot = place.piece(k, r, core)
        landed(s.rows.at[slot], s.rows_recv.at[slot], place)
        return slot

    for k in (1, 2, 3):
        mail.ship(s.rows.at[me], s.rows.at[me], s.rows_recv.at[me], ctx=place.column(k))

    def fan(k):
        slot = me if k == 0 else got(k, 0, a)
        forward(slot, place.right, place.left, place.sib)

    def relay(k):
        slot = got(k, 3, a)
        if k % 2 == 0:
            forward(slot, place.right)
        forward(slot, place.sib)
        slot = got(k, 1, a)
        if k % 2 == 1:
            forward(slot, place.left)
        forward(slot, place.sib)

    def end(k):
        forward(got(k, 2, a), place.sib)

    def gather_siblings(k):
        for r in range(4):
            got(k, r, 1 - a)

    order = (2, 1, 3, 0)

    def pieces_of(batch, r):
        return [place.piece(2 * batch + k, r, core) for k in range(2) for core in range(2)]

    def arrange(batch):
        for n, r in enumerate(order):
            stack = jnp.concatenate([s.rows[slot] for slot in pieces_of(batch, r)], axis=0)
            turned = jnp.dot(swap, stack, preferred_element_type=F32).astype(BF)
            for h in range(HEADS):
                for f in range(EXPERTS):
                    at = (f * HEADS + h) * HEAD
                    s.x[n * PIECE : (n + 1) * PIECE, at : at + HEAD] = turned[
                        h * PIECE : (h + 1) * PIECE, f * HEAD : (f + 1) * HEAD
                    ]

    def middle():
        x = s.x[...]
        g = lax.dot_general(x, s.w_gate[...], NT, preferred_element_type=F32)
        u = lax.dot_general(x, s.w_up[...], NT, preferred_element_type=F32)
        s.act[...] = (g / (1.0 + jnp.exp(-g)) * u).astype(BF)

    def down():
        def block(f, carry):
            at = pl.ds(pl.multiple_of(f * 512, 512), 512)
            s.y[:, at] = jnp.dot(s.act[...], s.w_down[:, at], preferred_element_type=F32).astype(BF)
            return carry

        lax.fori_loop(0, EXPERTS, block, 0)

    def hand_over(batch):
        for n, r in enumerate(order):
            tall = []
            for h in range(HEADS):
                at = [(f * HEADS + h) * HEAD for f in range(EXPERTS)]
                tall.append(
                    jnp.concatenate([s.y[n * PIECE : (n + 1) * PIECE, i : i + HEAD] for i in at], axis=1)
                )
            stack = jnp.concatenate(tall, axis=0)
            turned = jnp.dot(swap, stack, preferred_element_type=F32).astype(BF)
            for p, slot in enumerate(pieces_of(batch, r)):
                s.sums[slot] = turned[p * PIECE : (p + 1) * PIECE]
            for k in (2 * batch, 2 * batch + 1):
                slot = place.piece(k, r, 1 - a)
                mail.ship(s.sums.at[slot], s.beside.at[k * 4 + r2(r)], s.beside_recv.at[k * 4 + r2(r)], ctx=place.sib)

    def r2(r):
        return r

    def pair(k, r, *more):
        n = k * 4 + r
        landed(s.beside.at[n], s.beside_recv.at[n], place)
        total = s.sums[place.piece(k, r, a)].astype(F32) + s.beside[n].astype(F32)
        for ref, recv in more:
            landed(ref, recv, place)
            total = total + ref[...].astype(F32)
        slot = place.piece(k, r, a)
        s.sums[slot] = total.astype(BF)
        return s.sums.at[slot]

    def reduce_far(k):
        target = place.right if k % 2 == 0 else place.left
        mail.ship(pair(k, 2), s.relayed.at[k], s.relayed_recv.at[k], ctx=target)

    def reduce_near(k):
        extra = (s.relayed.at[k], s.relayed_recv.at[k])
        plain, joined = (3, 1) if k % 2 == 0 else (1, 3)
        for r in (plain, joined):
            more = (extra,) if r == joined else ()
            src = pair(k, r, *more)
            if r == 1:
                mail.ship(src, s.from_left.at[k], s.left_recv.at[k], ctx=place.right)
            else:
                mail.ship(src, s.from_right.at[k], s.right_recv.at[k], ctx=place.left)

    def reduce_own(k):
        src = pair(k, 0, (s.from_left.at[k], s.left_recv.at[k]), (s.from_right.at[k], s.right_recv.at[k]))
        if k > 0:
            mail.ship(src, s.from_z.at[k], s.z_recv.at[k], ctx=place.column(k))

    fan(0)
    fan(1)
    relay(0)
    relay(1)
    fan(2)
    fan(3)
    end(0)
    end(1)
    gather_siblings(0)
    gather_siblings(1)
    arrange(0)
    relay(2)
    relay(3)
    for copy in weights:
        copy.wait()
    middle()
    end(2)
    end(3)
    down()
    hand_over(0)
    reduce_far(0)
    reduce_far(1)
    gather_siblings(2)
    gather_siblings(3)
    arrange(1)
    reduce_near(0)
    reduce_near(1)
    middle()
    down()
    hand_over(1)
    reduce_far(2)
    reduce_far(3)
    reduce_own(1)
    reduce_near(2)
    reduce_near(3)
    reduce_own(0)
    reduce_own(2)
    reduce_own(3)
    total = s.sums[me].astype(F32)
    for k in (1, 2, 3):
        landed(s.from_z.at[k], s.z_recv.at[k], place)
        total = total + s.from_z[k].astype(F32)
    total = total.astype(BF)
    for f in range(EXPERTS):
        s.done[f] = total[:, f * HEAD : (f + 1) * HEAD]
    for j in range(1, EXPERTS):
        to = place.ek[j]
        mail.ship(s.done.at[to], s.home.at[e], s.home_recv.at[e], exp=to)
    s.home[e] = s.done[e]
    for j in range(1, EXPERTS):
        f = place.ek[j]
        landed(s.home.at[f], s.home_recv.at[f], place)
    back = jnp.concatenate([s.home[j] for j in range(EXPERTS)], axis=0)
    mixed = jnp.zeros((TALL, HEAD), F32)
    for k in range(2):
        gate = jnp.concatenate([gate_ref[:, k : k + 1]] * HEADS, axis=0)
        mixed = mixed + gate * jnp.dot(s.spread[k], back, preferred_element_type=F32)
    mail.drain()
    return mixed


def piece_buffers(count):
    return pltpu.VMEM((count, PIECE, WIDE), BF)


EXPERT_SCRATCH = dict(
    w_gate=pltpu.VMEM((HIDDEN, MODEL), BF),
    w_up=pltpu.VMEM((HIDDEN, MODEL), BF),
    w_down=pltpu.VMEM((HIDDEN, MODEL), BF),
    w_sem=pltpu.SemaphoreType.DMA((3,)),
    pick=pltpu.VMEM((EXPERTS, PIECE, HEAD), BF),
    picked=pltpu.VMEM((EXPERTS, PIECE, HEAD), BF),
    spread=pltpu.VMEM((2, TALL, EXPERTS * PIECE), BF),
    rows=piece_buffers(32),
    x=pltpu.VMEM((4 * PIECE, MODEL), BF),
    act=pltpu.VMEM((4 * PIECE, HIDDEN), BF),
    y=pltpu.VMEM((4 * PIECE, MODEL), BF),
    sums=piece_buffers(32),
    beside=piece_buffers(16),
    relayed=piece_buffers(4),
    from_left=piece_buffers(4),
    from_right=piece_buffers(4),
    from_z=piece_buffers(4),
    done=pltpu.VMEM((EXPERTS, PIECE, HEAD), BF),
    home=pltpu.VMEM((EXPERTS, PIECE, HEAD), BF),
    send=pltpu.SemaphoreType.DMA((80,)),
    picked_recv=pltpu.SemaphoreType.DMA((EXPERTS,)),
    rows_recv=pltpu.SemaphoreType.DMA((32,)),
    beside_recv=pltpu.SemaphoreType.DMA((16,)),
    relayed_recv=pltpu.SemaphoreType.DMA((4,)),
    left_recv=pltpu.SemaphoreType.DMA((4,)),
    right_recv=pltpu.SemaphoreType.DMA((4,)),
    z_recv=pltpu.SemaphoreType.DMA((4,)),
    home_recv=pltpu.SemaphoreType.DMA((EXPERTS,)),
)


def expert_kernel(hidden_ref, ids_ref, kept_ref, gate_ref, gain_ref, wg, wu, wd, out_ref, *scratch):
    s = types.SimpleNamespace(**dict(zip(EXPERT_SCRATCH, scratch)))
    place = Place()
    weights = fetch_weights(wg, wu, wd, s)
    for copy in weights:
        copy.start()
    greet(place, True)
    hidden = hidden_ref[...]
    mixed = experts(place, hidden, ids_ref, kept_ref, gate_ref, gain_ref, weights, s)
    out = (hidden.astype(F32) + mixed).astype(BF)
    for h in range(HEADS):
        out_ref[:, h * HEAD : (h + 1) * HEAD] = out[h * ROWS : (h + 1) * ROWS]


def expert_call(hidden, ids, kept, gates, gain, w_gate, w_up, w_down):
    vmem = pl.BlockSpec(memory_space=pltpu.VMEM)
    hbm = pl.BlockSpec(memory_space=pl.ANY)
    return pl.pallas_call(
        expert_kernel,
        out_shape=jax.ShapeDtypeStruct((ROWS, HEADS * HEAD), BF),
        in_specs=[vmem] * 5 + [hbm] * 3,
        out_specs=vmem,
        scratch_shapes=list(EXPERT_SCRATCH.values()),
        compiler_params=pltpu.CompilerParams(
            collective_id=1, has_side_effects=True, vmem_limit_bytes=48 * 2**20
        ),
        name="experts",
    )(hidden, ids, kept, gates, gain.astype(F32).reshape(32, HEAD), w_gate, w_up, w_down)


def body(
    residual_in,
    queries,
    context_key_cache,
    context_value_cache,
    query_pos,
    norm_gain,
    w_gate,
    w_up,
    w_down,
    expert_ids,
    kept_choices,
    gate_weights,
):
    hidden = attend_call(residual_in, queries, context_key_cache, context_value_cache, query_pos)
    return expert_call(
        hidden, expert_ids, kept_choices, gate_weights, norm_gain, w_gate, w_up, w_down
    )


def solution(mesh):
    in_specs = (
        P("ctx", "exp"),
        P("ctx", "exp"),
        P("ctx", "exp"),
        P("ctx", "exp"),
        P("ctx"),
        P(),
        P("exp", "ctx", None),
        P("exp", "ctx", None),
        P("exp", "ctx", None),
        P("ctx", None),
        P("ctx", None),
        P("ctx", None),
    )
    out_specs = P("ctx", "exp")
    return jax.shard_map(body, mesh=mesh, in_specs=in_specs, out_specs=out_specs, check_vma=False)
```

time: 498 us -> 126 us (0.25)
  waiting for transfers between devices: 254 us -> 0 us
  blocking collectives: 123 us -> 0 us
  Pallas kernels: 0 us -> 115 us
  matrix products: 51.1 us -> 0 us
  starting transfers between devices: 26.5 us -> 0 us
  other arithmetic: 20.9 us -> 0.7 us
  between operations: 14 us -> 0.03 us
    all_gather x3 -> x0, waiting for transfers between devices: 167 us -> none  [the longest x1 68.3 us: cycle_attention(): key_piece = lax.all_gather(context_key_cache, 'ctx', axis=0, tiled=True)]
    pallas_call x0 -> x2, Pallas kernels: none -> 115 us  [the longest x1 76.6 us: expert_call(): pl.pallas_call(expert_kernel, out_shape=jax.ShapeDtypeStruct((ROWS, HEADS...]
    reduce_scatter x1 -> x0, waiting for transfers between devices: 83.7 us -> none  [body(): lax.psum_scatter(returned.astype(jnp.bfloat16), 'exp', scatter_dimension=...]
    unnamed x1 -> x0, blocking collectives: 78.1 us -> none
    dot_general x7 -> x0, matrix products: 51.1 us -> none  [the longest x1 18 us: cycle_attention(): jnp.einsum('rkgd,nkd->rkgn', reshaped_array, key_piece.reshape(length, kv...]
    all_gather x1 -> x0, blocking collectives: 44.7 us -> none  [body(): full_rows = lax.all_gather(hidden, 'exp', axis=1, tiled=True)]
    unnamed x8 -> x0, starting transfers between devices: 26.2 us -> none
    reduce_sum x3 -> x0, other arithmetic: 15.1 us -> none  [the longest x1 14.9 us: softmax_update(): new_totals = jnp.sum(weights, axis=-1)]
  transfers between devices with their start and end apart: 12 -> 0, of which waited for: 6 -> 0; matrix products, arithmetic and copies ran while one was open for 8% -> 0% of each run, Pallas kernels for 0% -> 0%
where the time goes in v1:
time: 126 us; the launch traced here: 125 us
  Pallas kernels  115 us (91%)
  local copies, waits for them, and re-layouts  9.2 us (7%)
    pallas_call x1, Pallas kernels, expert_call(): pl.pallas_call(expert_kernel, out_shape=jax.ShapeDtypeStruct((ROWS, HEADS...  76.6 us
    pallas_call x1, Pallas kernels, attend_call(): pl.pallas_call(attend_kernel, out_shape=jax.ShapeDtypeStruct((TALL, HEAD)...  38.7 us
    unnamed x16, local copies, waits for them, and re-layouts  9.2 us

profile of v1, /device:TPU:2, one launch (start us, length us, event | category | flops | bytes accessed | tf_op | source)
XLA Modules:
  0.0 125.2 jit_solution(11389177906457823697)
XLA Ops:
  0.0 0.7 bitcast_convert_fusion.gain_ref
  0.7 0.8 copy.13.ids_ref
  1.5 0.8 copy.14.kept_ref
  2.2 0.8 copy.15.gate_ref
  3.0 0.0 copy-start.1
  3.0 0.9 copy-done.1
  4.0 0.0 copy-start.2
  4.0 0.9 copy-done.2
  4.9 0.0 copy-start.3
  4.9 0.8 copy-done.3
  5.7 0.0 copy-start.4
  5.7 0.8 copy-done.4
  6.6 0.0 copy-start.5
  6.6 0.7 copy-done.5
  7.2 38.7 %attend.1.hidden_ref = bf16[256,128]{1,0:T(8,128)(2,1)S(1)} custom-call(bf16[64,512]{1,0:T(8,128)(2,1)S(1)} %copy-done.3, bf16[64,512]{1,0:T(8,128)(2,1)S(1)} %copy-done.4, bf16[1024,128]{1,0:T(8,128)(2,1)S(1)} %copy-done.1, bf16[1024,128]{1,0:T(8,128)(2,1)S(1)} %copy-done.2, s32[1,64]{1,0:T(1,128)S(1)} %bitcast.4), custom_call_target="tpu_custom_call" | custom-call | tf_op jit(solution)/shard_map/attend/pallas_call | solution.py:358
  45.9 0.0 copy-start
  45.9 2.0 %copy-done = bf16[1,448,4096]{2,1,0:T(8,128)(2,1)S(1)} copy-done((bf16[1,448,4096]{2,1,0:T(8,128)(2,1)S(1)}, bf16[1,448,4096]{2,1,0:T(8,128)(2,1)}, u32[]{:S(2)}) %copy-start) | copy-done | bytes 3670040
  48.0 76.6 %experts.1 = bf16[64,512]{1,0:T(8,128)(2,1)S(1)} custom-call(bf16[256,128]{1,0:T(8,128)(2,1)S(1)} %attend.1.hidden_ref, s32[64,2]{1,0:T(8,128)S(1)} %copy.13.ids_ref, s32[64,2]{1,0:T(8,128)S(1)} %copy.14.kept_ref, f32[64,2]{1,0:T(8,128)S(1)} %copy.15.gate_ref, f32[32,128]{1,0:T(8,128)S(1)} %bitcast_convert_fusion.gain_ref, ...), custom_call_target="tpu_custom_call" | custom-call | tf_op jit(solution)/shard_map/experts/pallas_call | solution.py:713
  124.6 0.6 copy.17
Async XLA Ops:
  3.0 0.9 copy-start.1
  4.0 0.9 copy-start.2
  4.9 0.8 copy-start.3
  5.7 0.8 copy-start.4
  6.6 0.7 copy-start.5
  45.9 2.0 %copy-start = (bf16[1,448,4096]{2,1,0:T(8,128)(2,1)S(1)}, bf16[1,448,4096]{2,1,0:T(8,128)(2,1)}, u32[]{:S(2)}) copy-start(bf16[1,448,4096]{2,1,0:T(8,128)(2,1)} %wg.1) | copy-start | bytes 11010052

commit v2 on v1

v2 whole, which is shorter than its diff:
```python
import math
import types

import jax
import jax.numpy as jnp
from jax import lax
from jax.experimental import pallas as pl
from jax.experimental.pallas import tpu as pltpu
from jax.sharding import PartitionSpec as P

BF = jnp.bfloat16
F32 = jnp.float32
MESH = pl.DeviceIdType.MESH
NT = (((1,), (1,)), ((), ()))
NN = (((1,), (0,)), ((), ()))
HEAD = 128
ROWS = 64
HEADS = 4
TALL = ROWS * HEADS
KEYS = 1024
MODEL = 4096
HIDDEN = 448
EXPERTS = 8
SLOTS = 12
PIECE = SLOTS * HEADS
WIDE = EXPERTS * HEAD
NEG = -1e30
EPS = 1e-05
SCALE = HEAD ** (-0.5) * math.log2(math.e)


class Place:
    def __init__(self):
        self.me = lax.axis_index("ctx")
        self.e = lax.axis_index("exp")
        self.z = lax.div(self.me, 8)
        self.x = lax.rem(lax.div(self.me, 2), 4)
        self.a = lax.rem(self.me, 2)
        z = self.z
        self.zk = [z, z + 1 - 2 * lax.rem(z, 2), z + 2 - 4 * lax.div(z, 2), 3 - z]
        self.xr = [self.x] + [lax.rem(self.x + r, 4) for r in (1, 2, 3)]
        self.sib = self.spot(self.z, self.x, 1 - self.a)
        self.right = self.spot(self.z, self.xr[1], self.a)
        self.left = self.spot(self.z, self.xr[3], self.a)
        self.far = self.spot(self.z, self.xr[2], self.a)
        self.ek = [lax.rem(self.e + j, EXPERTS) for j in range(EXPERTS)]

    def spot(self, z, x, a):
        return z * 8 + x * 2 + a

    def piece(self, k, r, a):
        return self.spot(self.zk[k], self.xr[r], a)

    def column(self, k):
        return self.spot(self.zk[k], self.x, self.a)


class Mail:
    def __init__(self, place, sems):
        self.place, self.sems, self.used, self.open = place, sems, 0, []

    def ship(self, ref, at, to_ref, to, recv, recv_at, ctx=None, exp=None):
        target = {"ctx": ctx} if exp is None else {"exp": exp}
        number = self.used
        self.used += 1

        def make():
            return pltpu.make_async_remote_copy(
                src_ref=ref.at[at],
                dst_ref=to_ref.at[to],
                send_sem=self.sems.at[number],
                recv_sem=recv.at[recv_at],
                device_id=target,
                device_id_type=MESH,
            )

        make().start()
        self.open.append(make)

    def drain(self):
        for make in self.open:
            make().wait_send()
        self.open = []


def landed(slot, recv_sem, place):
    pltpu.make_async_remote_copy(
        src_ref=slot,
        dst_ref=slot,
        send_sem=recv_sem,
        recv_sem=recv_sem,
        device_id={"ctx": place.sib},
        device_id_type=MESH,
    ).wait_recv()


def wide(x, times):
    return jnp.concatenate([x] * times, axis=1)


def upright(line):
    row = lax.broadcasted_iota(jnp.int32, (ROWS, ROWS), 0)
    col = lax.broadcasted_iota(jnp.int32, (ROWS, ROWS), 1)
    return jnp.sum(jnp.where(row == col, line, 0.0), axis=1, keepdims=True)


def greet(place):
    barrier = pltpu.get_barrier_semaphore()
    peers = [{"ctx": c} for c in (place.sib, place.right, place.left, place.far)]
    peers += [{"ctx": place.column(k)} for k in (1, 2, 3)]
    peers += [{"exp": place.ek[j]} for j in range(1, EXPERTS)]
    for peer in peers:
        pl.semaphore_signal(barrier, inc=1, device_id=peer, device_id_type=MESH)
    pl.semaphore_wait(barrier, len(peers))


def attention(place, s, local, aside):
    z, a = place.z, place.a
    mail = Mail(place, s.kv_send)
    units = [[x * 2, x * 2 + 1] for x in place.xr]
    own = [lax.select(a == 0, u[0], u[1]) for u in units]
    other = [lax.select(a == 0, u[1], u[0]) for u in units]
    mine = own[0]
    order = [own[0], other[0], own[3], own[1], other[3], other[1], own[2], other[2]]

    downs = [place.spot(z - k, place.x, a) for k in range(4)]
    ups = [z + k for k in range(4)]

    def q_copy(k):
        return pltpu.make_async_remote_copy(
            src_ref=s.qg.at[z],
            dst_ref=s.qg.at[z],
            send_sem=s.q_send.at[k],
            recv_sem=s.q_recv.at[z],
            device_id={"ctx": downs[k]},
            device_id_type=MESH,
        )

    def send(ref, sem, u, *targets):
        for target in targets:
            mail.ship(ref, u, ref, u, sem, u, ctx=target)

    def got_k(u):
        landed(s.kg.at[u], s.k_recv.at[u], place)

    def got_v(u):
        landed(s.vg.at[u], s.v_recv.at[u], place)

    local["k"].wait()
    send(s.kg, s.k_recv, mine, place.right, place.left, place.sib)
    local["q"].wait()
    for k in (1, 2, 3):

        @pl.when(z >= k)
        def _(k=k):
            q_copy(k).start()

    local["v"].wait()
    send(s.vg, s.v_recv, mine, place.right, place.left, place.sib)

    s.peak[...] = jnp.full((4 * TALL, HEAD), NEG, F32)
    s.acc[...] = jnp.zeros((4 * TALL, 2 * HEAD), F32)

    def prepare(zq):
        for h in range(HEADS):
            at = pl.ds(pl.multiple_of(zq * TALL + h * ROWS, ROWS), ROWS)
            s.q2[at, :] = s.qg[zq, :, h * HEAD : (h + 1) * HEAD]

    def update(rows, u, pos_col=None):
        scores = lax.dot_general(s.q2[rows], s.kg[u], NT, preferred_element_type=F32)
        if pos_col is not None:
            key = lax.broadcasted_iota(jnp.int32, (TALL, KEYS), 1).astype(F32)
            scores = jnp.where(key <= pos_col, scores, NEG)
        old = s.peak[rows]
        new = jnp.maximum(old, jnp.max(scores, axis=1, keepdims=True))
        probs = jnp.exp2((scores - wide(new, KEYS // HEAD)) * SCALE)
        shrink = jnp.exp2((old - new) * SCALE)
        lanes = sum(probs[:, i : i + HEAD] for i in range(0, KEYS, HEAD))
        add = jnp.dot(probs.astype(BF), s.vg[u], preferred_element_type=F32)
        s.acc[rows, :HEAD] = s.acc[rows, :HEAD] * shrink + add
        s.acc[rows, HEAD:] = s.acc[rows, HEAD:] * shrink + lanes
        s.peak[rows] = new

    prepare(z)
    here = pl.ds(pl.multiple_of(z * TALL, TALL), TALL)
    pos = s.pos[...].astype(F32) - (place.me * KEYS).astype(F32)
    update(here, mine, jnp.concatenate([upright(pos)] * HEADS, axis=0))
    for k in (1, 2, 3):

        @pl.when(z + k <= 3)
        def _(k=k):
            landed(s.qg.at[ups[k]], s.q_recv.at[ups[k]], place)
            prepare(ups[k])

    def arrivals(n):
        if n == 1:
            got_k(other[0])
            got_v(other[0])
        elif n == 2:
            aside()
            got_k(own[3])
            send(s.kg, s.k_recv, own[3], place.right, place.sib)
            got_k(own[1])
            send(s.kg, s.k_recv, own[1], place.sib)
            got_v(own[1])
            send(s.vg, s.v_recv, own[1], place.left, place.sib)
            got_v(own[3])
            send(s.vg, s.v_recv, own[3], place.sib)
        elif n == 4:
            got_k(other[3])
            got_v(other[3])
        elif n == 5:
            got_k(other[1])
            got_v(other[1])
        elif n == 6:
            got_k(own[2])
            send(s.kg, s.k_recv, own[2], place.sib)
            got_v(own[2])
            send(s.vg, s.v_recv, own[2], place.sib)
        elif n == 7:
            got_k(other[2])
            got_v(other[2])

    def step(i, carry):
        for n in (1, 2, 4, 5, 6, 7):

            @pl.when(i == n)
            def _(n=n):
                arrivals(n)

        u = order[0]
        for n in range(1, 8):
            u = jnp.where(i == n, order[n], u)
        first = z + (u >= mine).astype(jnp.int32)
        for n in range(4):

            @pl.when(first == n)
            def _(n=n):
                update(slice(n * TALL, 4 * TALL), u)

        return carry

    lax.fori_loop(0, 8, step, 0)

    eye_r = lax.broadcasted_iota(jnp.int32, (HEAD, HEAD), 0)
    eye_c = lax.broadcasted_iota(jnp.int32, (HEAD, HEAD), 1)
    eye = eye_r == eye_c

    def back(zq):
        def one(src, dst, send, recv):
            return pltpu.make_async_remote_copy(
                src_ref=src.at[zq],
                dst_ref=dst.at[z],
                send_sem=send.at[zq],
                recv_sem=recv.at[z],
                device_id={"ctx": place.spot(zq, place.x, a)},
                device_id_type=MESH,
            )

        return (
            one(s.o_out, s.o_in, s.o_send, s.o_recv),
            one(s.l_out, s.l_in, s.l_send, s.l_recv),
        )

    def finish(i, carry):
        zq = 3 - i
        rows = pl.ds(pl.multiple_of(zq * TALL, TALL), TALL)
        total = jnp.sum(s.acc[rows, HEAD:], axis=1, keepdims=True)
        s.o_out[zq] = (s.acc[rows, :HEAD] / total).astype(BF)
        level = s.peak[rows] * SCALE + jnp.log2(total)
        for half in range(2):
            block = level[half * HEAD : (half + 1) * HEAD]
            s.l_out[zq, half : half + 1, :] = jnp.sum(
                jnp.where(eye, block, 0.0), axis=0, keepdims=True
            )
        for copy in back(zq):
            copy.start()
        return carry

    lax.fori_loop(0, 3 - z, finish, 0)

    s.level[...] = s.peak[here] * SCALE
    s.mix[...] = s.acc[here, :HEAD]
    s.mass[...] = jnp.sum(s.acc[here, HEAD:], axis=1, keepdims=True) + jnp.zeros((TALL, HEAD), F32)
    for k in (1, 2, 3):

        @pl.when(z >= k)
        def _(k=k):
            zs = z - k
            landed(s.o_in.at[zs], s.o_recv.at[zs], place)
            landed(s.l_in.at[zs], s.l_recv.at[zs], place)
            spread = []
            for half in range(2):
                line = s.l_in[zs, half : half + 1, :]
                spread.append(jnp.sum(jnp.where(eye, line, 0.0), axis=1, keepdims=True))
            level = jnp.concatenate(spread, axis=0) + jnp.zeros((TALL, HEAD), F32)
            old = s.level[...]
            new = jnp.maximum(old, level)
            shrink, weight = jnp.exp2(old - new), jnp.exp2(level - new)
            s.mix[...] = s.mix[...] * shrink + weight * s.o_in[zs].astype(F32)
            s.mass[...] = s.mass[...] * shrink + weight
            s.level[...] = new

    def settle():
        for k in (1, 2, 3):

            @pl.when(z >= k)
            def _(k=k):
                q_copy(k).wait_send()

        def last(i, carry):
            for copy in back(3 - i):
                copy.wait_send()
            return carry

        lax.fori_loop(0, 3 - z, last, 0)
        mail.drain()

    return s.mix[...] / s.mass[...], settle


ATTEND_SCRATCH = dict(
    kg=pltpu.VMEM((8, KEYS, HEAD), BF),
    vg=pltpu.VMEM((8, KEYS, HEAD), BF),
    qg=pltpu.VMEM((4, ROWS, HEADS * HEAD), BF),
    q2=pltpu.VMEM((4 * TALL, HEAD), BF),
    peak=pltpu.VMEM((4 * TALL, HEAD), F32),
    acc=pltpu.VMEM((4 * TALL, 2 * HEAD), F32),
    level=pltpu.VMEM((TALL, HEAD), F32),
    mix=pltpu.VMEM((TALL, HEAD), F32),
    mass=pltpu.VMEM((TALL, HEAD), F32),
    o_out=pltpu.VMEM((4, TALL, HEAD), BF),
    o_in=pltpu.VMEM((4, TALL, HEAD), BF),
    l_out=pltpu.VMEM((4, 8, HEAD), F32),
    l_in=pltpu.VMEM((4, 8, HEAD), F32),
    kv_send=pltpu.SemaphoreType.DMA((16,)),
    q_send=pltpu.SemaphoreType.DMA((4,)),
    q_recv=pltpu.SemaphoreType.DMA((4,)),
    k_recv=pltpu.SemaphoreType.DMA((8,)),
    v_recv=pltpu.SemaphoreType.DMA((8,)),
    o_send=pltpu.SemaphoreType.DMA((4,)),
    o_recv=pltpu.SemaphoreType.DMA((4,)),
    l_send=pltpu.SemaphoreType.DMA((4,)),
    l_recv=pltpu.SemaphoreType.DMA((4,)),
)


def steps(index, edges):
    return sum((index >= edge).astype(jnp.int32) for edge in edges)


def slot_columns(ids_ref, kept_ref):
    lane = lax.broadcasted_iota(jnp.int32, (ROWS, HEAD), 1)
    flags = []
    for k in range(2):
        ids = upright(ids_ref[k : k + 1, :].astype(F32))
        kept = upright(kept_ref[k : k + 1, :].astype(F32))
        flags.append(((ids == lane.astype(F32)) & (kept == 1.0)).astype(F32))
    before = (
        lax.broadcasted_iota(jnp.int32, (ROWS, ROWS), 1)
        < lax.broadcasted_iota(jnp.int32, (ROWS, ROWS), 0)
    ).astype(F32)
    columns = []
    passed = jnp.zeros((1, HEAD), F32)
    for flag in flags:
        rank = passed + jnp.dot(before, flag, preferred_element_type=F32)
        passed = passed + jnp.sum(flag, axis=0, keepdims=True)
        slot = flag * (lane.astype(F32) * SLOTS + rank + 1.0)
        columns.append(jnp.sum(slot, axis=1, keepdims=True) - 1.0)
    return columns


def slot_and_head(index):
    expert = steps(index, range(PIECE, EXPERTS * PIECE, PIECE))
    within = index - expert * PIECE
    head = steps(within, range(SLOTS, PIECE, SLOTS))
    return (expert * SLOTS + within - head * SLOTS).astype(F32), head


def pick_rows(columns):
    shape = (EXPERTS * PIECE, TALL)
    slot, head = slot_and_head(lax.broadcasted_iota(jnp.int32, shape, 0))
    lane = lax.broadcasted_iota(jnp.int32, (ROWS, TALL), 1)
    group = steps(lane, range(ROWS, TALL, ROWS))
    same = lax.broadcasted_iota(jnp.int32, (ROWS, TALL), 0) == lane - group * ROWS
    hit = jnp.zeros(shape, F32)
    for column in columns:
        line = jnp.sum(jnp.where(same, column, 0.0), axis=0, keepdims=True)
        hit = hit + (line == slot).astype(F32)
    lanes = lax.broadcasted_iota(jnp.int32, shape, 1)
    hit = jnp.where(steps(lanes, range(ROWS, TALL, ROWS)) == head, hit, 0.0)
    return hit.astype(BF)


def place_rows(column):
    shape = (TALL, EXPERTS * PIECE)
    slot, head = slot_and_head(lax.broadcasted_iota(jnp.int32, shape, 1))
    tall = jnp.concatenate([column] * HEADS, axis=0)
    rows = lax.broadcasted_iota(jnp.int32, shape, 0)
    hit = (slot == tall) & (steps(rows, range(ROWS, TALL, ROWS)) == head)
    return hit.astype(F32).astype(BF)


def swap_matrix():
    side = 4 * PIECE
    row = lax.broadcasted_iota(jnp.int32, (side, side), 0)
    col = lax.broadcasted_iota(jnp.int32, (side, side), 1)
    first = steps(row, (PIECE, 2 * PIECE, 3 * PIECE))
    within = row - first * PIECE
    second = steps(within, (SLOTS, 2 * SLOTS, 3 * SLOTS))
    slot = within - second * SLOTS
    return (col == second * PIECE + first * SLOTS + slot).astype(F32).astype(BF)


def tables(s):
    columns = slot_columns(s.ids, s.kept)
    s.take[...] = pick_rows(columns)
    for k in range(2):
        s.spread[k] = place_rows(columns[k])
    s.swap[...] = swap_matrix()
    part = lax.broadcasted_iota(jnp.int32, (PIECE, HEAD), 0)
    part = steps(part, (SLOTS, 2 * SLOTS, 3 * SLOTS))
    for f in range(EXPERTS):
        gain = s.gain_in[f * HEADS : f * HEADS + 1, :].astype(F32)
        for h in range(1, HEADS):
            at = f * HEADS + h
            gain = jnp.where(part >= h, s.gain_in[at : at + 1, :].astype(F32), gain)
        s.gain[f] = gain


def experts(place, hidden, weights, s):
    a, e = place.a, place.e
    mail = Mail(place, s.send)

    chosen = jnp.dot(s.take[...], hidden, preferred_element_type=F32).astype(BF)
    for j in range(EXPERTS):
        s.pick[j] = chosen[j * PIECE : (j + 1) * PIECE]
    for j in range(1, EXPERTS):
        to = place.ek[j]
        mail.ship(s.pick, to, s.picked, e, s.picked_recv, e, exp=to)
    s.picked[e] = s.pick[e]
    ring = lax.broadcasted_iota(jnp.int32, (PIECE, PIECE), 0)
    ring = ring - SLOTS * steps(ring, (SLOTS, 2 * SLOTS, 3 * SLOTS))
    lap = lax.broadcasted_iota(jnp.int32, (PIECE, PIECE), 1)
    lap = lap - SLOTS * steps(lap, (SLOTS, 2 * SLOTS, 3 * SLOTS))
    alike = (ring == lap).astype(F32)
    for j in range(1, EXPERTS):
        f = place.ek[j]
        landed(s.picked.at[f], s.picked_recv.at[f], place)

    squares = jnp.zeros((PIECE, HEAD), F32)
    for f in range(EXPERTS):
        x = s.picked[f].astype(F32)
        squares = squares + x * x
    squares = jnp.sum(squares, axis=1, keepdims=True) + jnp.zeros((PIECE, HEAD), F32)
    total = jnp.dot(alike, squares, precision=lax.Precision.HIGHEST, preferred_element_type=F32)
    scale = lax.rsqrt(total / MODEL + EPS)
    me = place.me
    for f in range(EXPERTS):
        s.rows[me, :, f * HEAD : (f + 1) * HEAD] = (
            s.picked[f].astype(F32) * scale * s.gain[f]
        ).astype(BF)

    def forward(slot, *targets):
        for target in targets:
            mail.ship(s.rows, slot, s.rows, slot, s.rows_recv, slot, ctx=target)

    def got(k, r, core):
        slot = place.piece(k, r, core)
        landed(s.rows.at[slot], s.rows_recv.at[slot], place)
        return slot

    forward(me, place.column(2), place.column(1))

    def fan(k):
        slot = me if k == 0 else got(k, 0, a)
        if k == 2:
            forward(slot, place.column(1))
        forward(slot, place.right, place.left)
        if k >= 2:
            forward(slot, place.far)
        forward(slot, place.sib)

    def relay(k):
        slot = got(k, 3, a)
        if k == 0:
            forward(slot, place.right)
        forward(slot, place.sib)
        slot = got(k, 1, a)
        if k == 1:
            forward(slot, place.left)
        forward(slot, place.sib)

    def end(k):
        forward(got(k, 2, a), place.sib)

    def gather_siblings(k):
        for r in range(4):
            got(k, r, 1 - a)

    def groups(k):
        return [[(r, core) for r in pair_of for core in range(2)] for pair_of in ((2, 1), (3, 0))]

    def arrange(ks):
        for m, k in enumerate(ks):
            for n, group in enumerate(groups(k)):
                slots = [place.piece(k, r, core) for r, core in group]
                stack = jnp.concatenate([s.rows[slot] for slot in slots], axis=0)
                turned = jnp.dot(s.swap[...], stack, preferred_element_type=F32).astype(BF)
                top = (2 * m + n) * PIECE
                for h in range(HEADS):
                    for f in range(EXPERTS):
                        at = (f * HEADS + h) * HEAD
                        s.x[top : top + PIECE, at : at + HEAD] = turned[
                            h * PIECE : (h + 1) * PIECE, f * HEAD : (f + 1) * HEAD
                        ]

    def middle(task):
        s.g[...] = lax.dot_general(s.x[...], s.w_gate[...], NT, preferred_element_type=F32)
        task()
        u = lax.dot_general(s.x[...], s.w_up[...], NT, preferred_element_type=F32)
        g = s.g[...]
        s.act[...] = (g / (1.0 + jnp.exp(-g)) * u).astype(BF)

    def down(task):
        for at in range(0, MODEL, 1024):
            cols = slice(at, at + 1024)
            s.y[:, cols] = jnp.dot(s.act[...], s.w_down[:, cols], preferred_element_type=F32).astype(BF)
            if at == 1024:
                task()

    def hand_over(m, k):
        for n, group in enumerate(groups(k)):
            top = (2 * m + n) * PIECE
            tall = []
            for h in range(HEADS):
                at = [(f * HEADS + h) * HEAD for f in range(EXPERTS)]
                tall.append(
                    jnp.concatenate([s.y[top : top + PIECE, i : i + HEAD] for i in at], axis=1)
                )
            stack = jnp.concatenate(tall, axis=0)
            turned = jnp.dot(s.swap[...], stack, preferred_element_type=F32).astype(BF)
            for p, (r, core) in enumerate(group):
                s.sums[place.piece(k, r, core)] = turned[p * PIECE : (p + 1) * PIECE]
            for r in dict.fromkeys(r for r, _ in group):
                slot, to = place.piece(k, r, 1 - a), k * 4 + r
                mail.ship(s.sums, slot, s.beside, to, s.beside_recv, to, ctx=place.sib)

    def pair(k, r, *more):
        n = k * 4 + r
        landed(s.beside.at[n], s.beside_recv.at[n], place)
        total = s.sums[place.piece(k, r, a)].astype(F32) + s.beside[n].astype(F32)
        for ref, recv in more:
            landed(ref, recv, place)
            total = total + ref[...].astype(F32)
        slot = place.piece(k, r, a)
        s.sums[slot] = total.astype(BF)
        return slot

    def reduce_far(k):
        target = place.right if k % 2 == 0 else place.left
        mail.ship(s.sums, pair(k, 2), s.relayed, k, s.relayed_recv, k, ctx=target)

    def reduce_near(k, joined):
        r = 1 if (k % 2 == 0) == joined else 3
        more = ((s.relayed.at[k], s.relayed_recv.at[k]),) if joined else ()
        src = pair(k, r, *more)
        if r == 1:
            mail.ship(s.sums, src, s.from_left, k, s.left_recv, k, ctx=place.right)
        else:
            mail.ship(s.sums, src, s.from_right, k, s.right_recv, k, ctx=place.left)

    def reduce_own(k, *more):
        sides = ((s.from_left.at[k], s.left_recv.at[k]), (s.from_right.at[k], s.right_recv.at[k]))
        src = pair(k, 0, *sides, *more)
        if k > 0:
            mail.ship(s.sums, src, s.from_z, k, s.z_recv, k, ctx=place.column(k))

    def z_in(k):
        return (s.from_z.at[k], s.z_recv.at[k])

    def work(ks, *tasks):
        for k in ks:
            gather_siblings(k)
        arrange(ks)
        if ks[0] == 0:
            for copy in weights:
                copy.wait()
        middle(tasks[0])
        tasks[1]()
        down(tasks[2])
        for m, k in reversed(list(enumerate(ks))):
            hand_over(m, k)

    def send_first(*ks):
        for k in ks:
            reduce_far(k)
        for k in ks:
            reduce_near(k, False)

    fan(0)
    fan(1)
    relay(0)
    fan(2)
    relay(1)
    fan(3)
    end(0)
    end(1)
    work((0, 1), lambda: relay(2), lambda: relay(3), lambda: end(2))
    end(3)
    send_first(1, 0)
    work((2, 3), lambda: reduce_near(1, True), lambda: reduce_near(0, True), lambda: reduce_own(1))
    send_first(3, 2)
    reduce_own(0)
    reduce_near(3, True)
    reduce_near(2, True)
    reduce_own(3)
    reduce_own(2)
    total = s.sums[me].astype(F32)
    for k in (1, 2, 3):
        landed(*z_in(k), place)
        total = total + s.from_z[k].astype(F32)
    total = total.astype(BF)
    for f in range(EXPERTS):
        s.done[f] = total[:, f * HEAD : (f + 1) * HEAD]
    for j in range(1, EXPERTS):
        to = place.ek[j]
        mail.ship(s.done, to, s.home, e, s.home_recv, e, exp=to)
    s.home[e] = s.done[e]
    for j in range(1, EXPERTS):
        f = place.ek[j]
        landed(s.home.at[f], s.home_recv.at[f], place)
    back = jnp.concatenate([s.home[j] for j in range(EXPERTS)], axis=0)
    mixed = jnp.zeros((TALL, HEAD), F32)
    for k in range(2):
        gate = jnp.concatenate([upright(s.gates[k : k + 1, :])] * HEADS, axis=0)
        mixed = mixed + gate * jnp.dot(s.spread[k], back, preferred_element_type=F32)
    return mixed, mail.drain


def piece_buffers(count):
    return pltpu.VMEM((count, PIECE, WIDE), BF)


EXPERT_SCRATCH = dict(
    w_gate=pltpu.VMEM((HIDDEN, MODEL), BF),
    w_up=pltpu.VMEM((HIDDEN, MODEL), BF),
    w_down=pltpu.VMEM((HIDDEN, MODEL), BF),
    take=pltpu.VMEM((EXPERTS * PIECE, TALL), BF),
    swap=pltpu.VMEM((4 * PIECE, 4 * PIECE), BF),
    gain=pltpu.VMEM((EXPERTS, PIECE, HEAD), F32),
    pick=pltpu.VMEM((EXPERTS, PIECE, HEAD), BF),
    picked=pltpu.VMEM((EXPERTS, PIECE, HEAD), BF),
    spread=pltpu.VMEM((2, TALL, EXPERTS * PIECE), BF),
    rows=piece_buffers(32),
    x=pltpu.VMEM((4 * PIECE, MODEL), BF),
    g=pltpu.VMEM((4 * PIECE, HIDDEN), F32),
    act=pltpu.VMEM((4 * PIECE, HIDDEN), BF),
    y=pltpu.VMEM((4 * PIECE, MODEL), BF),
    sums=piece_buffers(32),
    beside=piece_buffers(16),
    relayed=piece_buffers(4),
    from_left=piece_buffers(4),
    from_right=piece_buffers(4),
    from_z=piece_buffers(4),
    done=pltpu.VMEM((EXPERTS, PIECE, HEAD), BF),
    home=pltpu.VMEM((EXPERTS, PIECE, HEAD), BF),
    send=pltpu.SemaphoreType.DMA((80,)),
    picked_recv=pltpu.SemaphoreType.DMA((EXPERTS,)),
    rows_recv=pltpu.SemaphoreType.DMA((32,)),
    beside_recv=pltpu.SemaphoreType.DMA((16,)),
    relayed_recv=pltpu.SemaphoreType.DMA((4,)),
    left_recv=pltpu.SemaphoreType.DMA((4,)),
    right_recv=pltpu.SemaphoreType.DMA((4,)),
    z_recv=pltpu.SemaphoreType.DMA((4,)),
    home_recv=pltpu.SemaphoreType.DMA((EXPERTS,)),
)


LOCAL_SCRATCH = dict(
    res=pltpu.VMEM((ROWS, HEADS * HEAD), BF),
    hidden=pltpu.VMEM((TALL, HEAD), BF),
    pos=pltpu.VMEM((1, ROWS), jnp.int32),
    gain_in=pltpu.VMEM((32, HEAD), BF),
    ids=pltpu.VMEM((2, ROWS), jnp.int32),
    kept=pltpu.VMEM((2, ROWS), jnp.int32),
    gates=pltpu.VMEM((2, ROWS), F32),
    local_sem=pltpu.SemaphoreType.DMA((12,)),
)
SCRATCH = ATTEND_SCRATCH | EXPERT_SCRATCH | LOCAL_SCRATCH


def layer_kernel(res, q, key, value, pos, gain, wg, wu, wd, ids, kept, gates, out_ref, *scratch):
    s = types.SimpleNamespace(**dict(zip(SCRATCH, scratch)))
    place = Place()
    mine = place.x * 2 + place.a
    moves = dict(
        k=(key, s.kg.at[mine]),
        v=(value, s.vg.at[mine]),
        q=(q, s.qg.at[place.z]),
        pos=(pos, s.pos),
        ids=(ids, s.ids),
        kept=(kept, s.kept),
        gates=(gates, s.gates),
        gain=(gain, s.gain_in),
        res=(res, s.res),
        wg=(wg.at[0], s.w_gate),
        wu=(wu.at[0], s.w_up),
        wd=(wd.at[0], s.w_down),
    )
    local = {
        name: pltpu.make_async_copy(src, dst, s.local_sem.at[i])
        for i, (name, (src, dst)) in enumerate(moves.items())
    }
    for copy in local.values():
        copy.start()
    greet(place)

    for name in ("pos",):
        local[name].wait()

    def aside():
        for name in ("ids", "kept", "gates", "gain", "res"):
            local[name].wait()
        tables(s)

    attended, settle = attention(place, s, local, aside)
    tall = []
    for h in range(HEADS):
        res_h = s.res[:, h * HEAD : (h + 1) * HEAD].astype(F32)
        tall.append((res_h + attended[h * ROWS : (h + 1) * ROWS]).astype(BF))
    hidden = jnp.concatenate(tall, axis=0)
    s.hidden[...] = hidden
    weights = [local[name] for name in ("wg", "wu", "wd")]
    mixed, drain = experts(place, hidden, weights, s)
    for h in range(HEADS):
        rows = slice(h * ROWS, (h + 1) * ROWS)
        out_ref[:, h * HEAD : (h + 1) * HEAD] = (s.hidden[rows].astype(F32) + mixed[rows]).astype(BF)
    settle()
    drain()


def body(
    residual_in,
    queries,
    context_key_cache,
    context_value_cache,
    query_pos,
    norm_gain,
    w_gate,
    w_up,
    w_down,
    expert_ids,
    kept_choices,
    gate_weights,
):
    any_spec = pl.BlockSpec(memory_space=pl.ANY)
    return pl.pallas_call(
        layer_kernel,
        out_shape=jax.ShapeDtypeStruct((ROWS, HEADS * HEAD), BF),
        in_specs=[any_spec] * 12,
        out_specs=pl.BlockSpec(memory_space=pltpu.VMEM),
        scratch_shapes=list(SCRATCH.values()),
        compiler_params=pltpu.CompilerParams(
            collective_id=0, has_side_effects=True, vmem_limit_bytes=56 * 2**20
        ),
        name="layer",
    )(
        residual_in,
        queries,
        context_key_cache,
        context_value_cache,
        query_pos.reshape(1, ROWS),
        norm_gain.reshape(32, HEAD),
        w_gate,
        w_up,
        w_down,
        expert_ids.T,
        kept_choices.T,
        gate_weights.T,
    )


def solution(mesh):
    in_specs = (
        P("ctx", "exp"),
        P("ctx", "exp"),
        P("ctx", "exp"),
        P("ctx", "exp"),
        P("ctx"),
        P(),
        P("exp", "ctx", None),
        P("exp", "ctx", None),
        P("exp", "ctx", None),
        P("ctx", None),
        P("ctx", None),
        P("ctx", None),
    )
    out_specs = P("ctx", "exp")
    return jax.shard_map(body, mesh=mesh, in_specs=in_specs, out_specs=out_specs, check_vma=False)
```

time: 126 us -> 109 us (0.87)
  local copies, waits for them, and re-layouts: 9.2 us -> 1.47 us
  Pallas kernels: 115 us -> 108 us
    unnamed x16 -> x1, local copies, waits for them, and re-layouts: 9.2 us -> 1.47 us
    pallas_call x2 -> x1, Pallas kernels: 115 us -> 108 us  [body(): pl.pallas_call(layer_kernel, out_shape=jax.ShapeDtypeStruct((ROWS, HEADS...]
where the time goes in v2:
time: 109 us
  Pallas kernels  108 us (99%)
  local copies, waits for them, and re-layouts  1.47 us (1%)
    pallas_call x1, Pallas kernels, body(): pl.pallas_call(layer_kernel, out_shape=jax.ShapeDtypeStruct((ROWS, HEADS...  108 us

profile of v2, /device:TPU:2, one launch (start us, length us, event | category | flops | bytes accessed | tf_op | source)
XLA Modules:
  0.0 109.1 jit_solution(15217773878584378937)
XLA Ops:
  0.0 107.6 %layer.1 = bf16[64,512]{1,0:T(8,128)(2,1)} custom-call(bf16[64,512]{1,0:T(8,128)(2,1)} %res.1, bf16[64,512]{1,0:T(8,128)(2,1)} %q.1, bf16[1024,128]{1,0:T(8,128)(2,1)} %key.1, bf16[1024,128]{1,0:T(8,128)(2,1)} %value.1, s32[1,64]{1,0:T(1,128)} %bitcast.9, bf16[32,128]{1,0:T(8,128)(2,1)} %bitcast.5, bf16[1,448,4096]{2,1,0:T(8,128)(2,1)} %wg.1, ...), custom_call_target="tpu_custom_call" | custom-call | tf_op jit(solution)/shard_map/layer/pallas_call | solution.py:758
  107.6 1.5 %copy.14 = bf16[64,512]{1,0:T(8,128)(2,1)} copy(bf16[64,512]{1,0:T(8,128)(2,1)} %layer.1) | data formatting | bytes 131072

commit v3 on v2

--- a/solution.py
+++ b/solution.py
@@ -26,6 +26,7 @@
 WIDE = EXPERTS * HEAD
 NEG = -1e30
 EPS = 1e-05
+DIRECT = (2, 3)
 SCALE = HEAD ** (-0.5) * math.log2(math.e)
 
 
@@ -60,7 +61,7 @@
         self.place, self.sems, self.used, self.open = place, sems, 0, []
 
     def ship(self, ref, at, to_ref, to, recv, recv_at, ctx=None, exp=None):
-        target = {"ctx": ctx} if exp is None else {"exp": exp}
+        target = {name: to_ for name, to_ in (("ctx", ctx), ("exp", exp)) if to_ is not None}
         number = self.used
         self.used += 1
 
@@ -107,8 +108,12 @@
 def greet(place):
     barrier = pltpu.get_barrier_semaphore()
     peers = [{"ctx": c} for c in (place.sib, place.right, place.left, place.far)]
-    peers += [{"ctx": place.column(k)} for k in (1, 2, 3)]
-    peers += [{"exp": place.ek[j]} for j in range(1, EXPERTS)]
+    peers += [
+        {"ctx": place.column(k), "exp": place.ek[j]}
+        for k in range(4)
+        for j in range(EXPERTS)
+        if k or j
+    ]
     for peer in peers:
         pl.semaphore_signal(barrier, inc=1, device_id=peer, device_id_type=MESH)
     pl.semaphore_wait(barrier, len(peers))
@@ -477,17 +482,17 @@
         if k == 2:
             forward(slot, place.column(1))
         forward(slot, place.right, place.left)
-        if k >= 2:
+        if k in DIRECT:
             forward(slot, place.far)
         forward(slot, place.sib)
 
     def relay(k):
         slot = got(k, 3, a)
-        if k == 0:
+        if k % 2 == 0 and k not in DIRECT:
             forward(slot, place.right)
         forward(slot, place.sib)
         slot = got(k, 1, a)
-        if k == 1:
+        if k % 2 == 1 and k not in DIRECT:
             forward(slot, place.left)
         forward(slot, place.sib)
 
@@ -570,14 +575,18 @@
         else:
             mail.ship(s.sums, src, s.from_right, k, s.right_recv, k, ctx=place.left)
 
-    def reduce_own(k, *more):
+    def reduce_own(k):
         sides = ((s.from_left.at[k], s.left_recv.at[k]), (s.from_right.at[k], s.right_recv.at[k]))
-        src = pair(k, 0, *sides, *more)
-        if k > 0:
-            mail.ship(s.sums, src, s.from_z, k, s.z_recv, k, ctx=place.column(k))
-
-    def z_in(k):
-        return (s.from_z.at[k], s.z_recv.at[k])
+        total = s.sums[pair(k, 0, *sides)]
+        for f in range(EXPERTS):
+            s.done[k, f] = total[:, f * HEAD : (f + 1) * HEAD]
+        for j in reversed(range(EXPERTS)):
+            to = place.ek[j]
+            if k or j:
+                where = dict(ctx=place.column(k), exp=to)
+                mail.ship(s.done, (k, to), s.home, (k, e), s.home_recv, k * EXPERTS + e, **where)
+            else:
+                s.home[0, e] = s.done[0, e]
 
     def work(ks, *tasks):
         for k in ks:
@@ -598,6 +607,9 @@
         for k in ks:
             reduce_near(k, False)
 
+    def idle():
+        return None
+
     fan(0)
     fan(1)
     relay(0)
@@ -606,35 +618,33 @@
     fan(3)
     end(0)
     end(1)
-    work((0, 1), lambda: relay(2), lambda: relay(3), lambda: end(2))
-    end(3)
+    relay(2)
+    work((0, 1), lambda: relay(3), lambda: end(2), lambda: end(3))
     send_first(1, 0)
-    work((2, 3), lambda: reduce_near(1, True), lambda: reduce_near(0, True), lambda: reduce_own(1))
+    work((2, 3), idle, idle, idle)
     send_first(3, 2)
-    reduce_own(0)
+    reduce_near(1, True)
+    reduce_near(0, True)
     reduce_near(3, True)
     reduce_near(2, True)
+    reduce_own(1)
+    reduce_own(0)
     reduce_own(3)
     reduce_own(2)
-    total = s.sums[me].astype(F32)
-    for k in (1, 2, 3):
-        landed(*z_in(k), place)
-        total = total + s.from_z[k].astype(F32)
-    total = total.astype(BF)
-    for f in range(EXPERTS):
-        s.done[f] = total[:, f * HEAD : (f + 1) * HEAD]
-    for j in range(1, EXPERTS):
-        to = place.ek[j]
-        mail.ship(s.done, to, s.home, e, s.home_recv, e, exp=to)
-    s.home[e] = s.done[e]
-    for j in range(1, EXPERTS):
-        f = place.ek[j]
-        landed(s.home.at[f], s.home_recv.at[f], place)
-    back = jnp.concatenate([s.home[j] for j in range(EXPERTS)], axis=0)
+    gates = [
+        jnp.concatenate([upright(s.gates[k : k + 1, :])] * HEADS, axis=0) for k in range(2)
+    ]
+    for k in (1, 0, 3, 2):
+        for j in range(EXPERTS):
+            if k or j:
+                f = place.ek[j]
+                landed(s.home.at[k, f], s.home_recv.at[k * EXPERTS + f], place)
+    back = jnp.concatenate(
+        [sum(s.home[k, j].astype(F32) for k in range(4)).astype(BF) for j in range(EXPERTS)], axis=0
+    )
     mixed = jnp.zeros((TALL, HEAD), F32)
     for k in range(2):
-        gate = jnp.concatenate([upright(s.gates[k : k + 1, :])] * HEADS, axis=0)
-        mixed = mixed + gate * jnp.dot(s.spread[k], back, preferred_element_type=F32)
+        mixed = mixed + gates[k] * jnp.dot(s.spread[k], back, preferred_element_type=F32)
     return mixed, mail.drain
 
 
@@ -662,18 +672,16 @@
     relayed=piece_buffers(4),
     from_left=piece_buffers(4),
     from_right=piece_buffers(4),
-    from_z=piece_buffers(4),
-    done=pltpu.VMEM((EXPERTS, PIECE, HEAD), BF),
-    home=pltpu.VMEM((EXPERTS, PIECE, HEAD), BF),
-    send=pltpu.SemaphoreType.DMA((80,)),
+    done=pltpu.VMEM((4, EXPERTS, PIECE, HEAD), BF),
+    home=pltpu.VMEM((4, EXPERTS, PIECE, HEAD), BF),
+    send=pltpu.SemaphoreType.DMA((112,)),
     picked_recv=pltpu.SemaphoreType.DMA((EXPERTS,)),
     rows_recv=pltpu.SemaphoreType.DMA((32,)),
     beside_recv=pltpu.SemaphoreType.DMA((16,)),
     relayed_recv=pltpu.SemaphoreType.DMA((4,)),
     left_recv=pltpu.SemaphoreType.DMA((4,)),
     right_recv=pltpu.SemaphoreType.DMA((4,)),
-    z_recv=pltpu.SemaphoreType.DMA((4,)),
-    home_recv=pltpu.SemaphoreType.DMA((EXPERTS,)),
+    home_recv=pltpu.SemaphoreType.DMA((4 * EXPERTS,)),
 )
 
 

time: 109 us -> 102 us (0.936); the launches traced: 109 us -> 100 us
  Pallas kernels: 108 us -> 98.8 us
    pallas_call x1, Pallas kernels: 108 us -> 98.8 us  [body(): pl.pallas_call(layer_kernel, out_shape=jax.ShapeDtypeStruct((ROWS, HEADS...]
where the time goes in v3:
time: 102 us; the launch traced here: 100 us
  Pallas kernels  98.8 us (97%)
  local copies, waits for them, and re-layouts  1.47 us (1%)
    pallas_call x1, Pallas kernels, body(): pl.pallas_call(layer_kernel, out_shape=jax.ShapeDtypeStruct((ROWS, HEADS...  98.8 us

profile of v3, /device:TPU:2, one launch (start us, length us, event | category | flops | bytes accessed | tf_op | source)
XLA Modules:
  0.0 100.2 jit_solution(2166063236309167320)
XLA Ops:
  0.0 98.8 %layer.1 = bf16[64,512]{1,0:T(8,128)(2,1)} custom-call(bf16[64,512]{1,0:T(8,128)(2,1)} %res.1, bf16[64,512]{1,0:T(8,128)(2,1)} %q.1, bf16[1024,128]{1,0:T(8,128)(2,1)} %key.1, bf16[1024,128]{1,0:T(8,128)(2,1)} %value.1, s32[1,64]{1,0:T(1,128)} %bitcast.9, bf16[32,128]{1,0:T(8,128)(2,1)} %bitcast.5, bf16[1,448,4096]{2,1,0:T(8,128)(2,1)} %wg.1, ...), custom_call_target="tpu_custom_call" | custom-call | tf_op jit(solution)/shard_map/layer/pallas_call | solution.py:766
  98.8 1.5 %copy.14 = bf16[64,512]{1,0:T(8,128)(2,1)} copy(bf16[64,512]{1,0:T(8,128)(2,1)} %layer.1) | data formatting | bytes 131072

commit v4 on v3

--- a/solution.py
+++ b/solution.py
@@ -27,6 +27,7 @@
 NEG = -1e30
 EPS = 1e-05
 DIRECT = (2, 3)
+STRAIGHT = (0, 1)
 SCALE = HEAD ** (-0.5) * math.log2(math.e)
 
 
@@ -145,6 +146,12 @@
         for target in targets:
             mail.ship(ref, u, ref, u, sem, u, ctx=target)
 
+    def first_half(u):
+        return (u, pl.ds(0, KEYS // 2))
+
+    def last_half(u):
+        return (u, pl.ds(KEYS // 2, KEYS // 2))
+
     def got_k(u):
         landed(s.kg.at[u], s.k_recv.at[u], place)
 
@@ -204,12 +211,16 @@
         elif n == 2:
             aside()
             got_k(own[3])
-            send(s.kg, s.k_recv, own[3], place.right, place.sib)
+            mail.ship(s.kg, first_half(own[3]), s.kg, first_half(own[3]), s.k_recv, own[3], ctx=place.right)
+            send(s.kg, s.k_recv, own[3], place.sib)
             got_k(own[1])
+            mail.ship(s.kg, last_half(own[1]), s.kg, last_half(own[1]), s.k_half, own[1], ctx=place.left)
             send(s.kg, s.k_recv, own[1], place.sib)
             got_v(own[1])
-            send(s.vg, s.v_recv, own[1], place.left, place.sib)
+            mail.ship(s.vg, last_half(own[1]), s.vg, last_half(own[1]), s.v_half, own[1], ctx=place.left)
+            send(s.vg, s.v_recv, own[1], place.sib)
             got_v(own[3])
+            mail.ship(s.vg, first_half(own[3]), s.vg, first_half(own[3]), s.v_recv, own[3], ctx=place.right)
             send(s.vg, s.v_recv, own[3], place.sib)
         elif n == 4:
             got_k(other[3])
@@ -218,10 +229,13 @@
             got_k(other[1])
             got_v(other[1])
         elif n == 6:
-            got_k(own[2])
-            send(s.kg, s.k_recv, own[2], place.sib)
-            got_v(own[2])
-            send(s.vg, s.v_recv, own[2], place.sib)
+            far = own[2]
+            landed(s.kg.at[first_half(far)], s.k_recv.at[far], place)
+            landed(s.kg.at[last_half(far)], s.k_half.at[far], place)
+            send(s.kg, s.k_recv, far, place.sib)
+            landed(s.vg.at[first_half(far)], s.v_recv.at[far], place)
+            landed(s.vg.at[last_half(far)], s.v_half.at[far], place)
+            send(s.vg, s.v_recv, far, place.sib)
         elif n == 7:
             got_k(other[2])
             got_v(other[2])
@@ -343,6 +357,8 @@
     q_recv=pltpu.SemaphoreType.DMA((4,)),
     k_recv=pltpu.SemaphoreType.DMA((8,)),
     v_recv=pltpu.SemaphoreType.DMA((8,)),
+    k_half=pltpu.SemaphoreType.DMA((8,)),
+    v_half=pltpu.SemaphoreType.DMA((8,)),
     o_send=pltpu.SemaphoreType.DMA((4,)),
     o_recv=pltpu.SemaphoreType.DMA((4,)),
     l_send=pltpu.SemaphoreType.DMA((4,)),
@@ -563,20 +579,30 @@
         return slot
 
     def reduce_far(k):
-        target = place.right if k % 2 == 0 else place.left
-        mail.ship(s.sums, pair(k, 2), s.relayed, k, s.relayed_recv, k, ctx=target)
+        src = pair(k, 2)
+        if k in STRAIGHT:
+            mail.ship(s.sums, src, s.from_far, k, s.far_recv, k, ctx=place.far)
+        else:
+            target = place.right if k % 2 == 0 else place.left
+            mail.ship(s.sums, src, s.relayed, k, s.relayed_recv, k, ctx=target)
 
     def reduce_near(k, joined):
-        r = 1 if (k % 2 == 0) == joined else 3
+        if k in STRAIGHT:
+            todo = () if joined else (1, 3)
+        else:
+            todo = (1 if (k % 2 == 0) == joined else 3,)
         more = ((s.relayed.at[k], s.relayed_recv.at[k]),) if joined else ()
-        src = pair(k, r, *more)
-        if r == 1:
-            mail.ship(s.sums, src, s.from_left, k, s.left_recv, k, ctx=place.right)
-        else:
-            mail.ship(s.sums, src, s.from_right, k, s.right_recv, k, ctx=place.left)
+        for r in todo:
+            src = pair(k, r, *more)
+            if r == 1:
+                mail.ship(s.sums, src, s.from_left, k, s.left_recv, k, ctx=place.right)
+            else:
+                mail.ship(s.sums, src, s.from_right, k, s.right_recv, k, ctx=place.left)
 
     def reduce_own(k):
         sides = ((s.from_left.at[k], s.left_recv.at[k]), (s.from_right.at[k], s.right_recv.at[k]))
+        if k in STRAIGHT:
+            sides += ((s.from_far.at[k], s.far_recv.at[k]),)
         total = s.sums[pair(k, 0, *sides)]
         for f in range(EXPERTS):
             s.done[k, f] = total[:, f * HEAD : (f + 1) * HEAD]
@@ -619,7 +645,8 @@
     end(0)
     end(1)
     relay(2)
-    work((0, 1), lambda: relay(3), lambda: end(2), lambda: end(3))
+    work((0, 1), lambda: relay(3), lambda: end(2), idle)
+    end(3)
     send_first(1, 0)
     work((2, 3), idle, idle, idle)
     send_first(3, 2)
@@ -634,13 +661,20 @@
     gates = [
         jnp.concatenate([upright(s.gates[k : k + 1, :])] * HEADS, axis=0) for k in range(2)
     ]
-    for k in (1, 0, 3, 2):
+    def home_in(k):
         for j in range(EXPERTS):
             if k or j:
                 f = place.ek[j]
                 landed(s.home.at[k, f], s.home_recv.at[k * EXPERTS + f], place)
+
+    home_in(1)
+    home_in(0)
+    early = [s.home[0, j].astype(F32) + s.home[1, j].astype(F32) for j in range(EXPERTS)]
+    home_in(3)
+    home_in(2)
     back = jnp.concatenate(
-        [sum(s.home[k, j].astype(F32) for k in range(4)).astype(BF) for j in range(EXPERTS)], axis=0
+        [(early[j] + (s.home[2, j].astype(F32) + s.home[3, j].astype(F32))).astype(BF) for j in range(EXPERTS)],
+        axis=0,
     )
     mixed = jnp.zeros((TALL, HEAD), F32)
     for k in range(2):
@@ -672,6 +706,7 @@
     relayed=piece_buffers(4),
     from_left=piece_buffers(4),
     from_right=piece_buffers(4),
+    from_far=piece_buffers(4),
     done=pltpu.VMEM((4, EXPERTS, PIECE, HEAD), BF),
     home=pltpu.VMEM((4, EXPERTS, PIECE, HEAD), BF),
     send=pltpu.SemaphoreType.DMA((112,)),
@@ -681,6 +716,7 @@
     relayed_recv=pltpu.SemaphoreType.DMA((4,)),
     left_recv=pltpu.SemaphoreType.DMA((4,)),
     right_recv=pltpu.SemaphoreType.DMA((4,)),
+    far_recv=pltpu.SemaphoreType.DMA((4,)),
     home_recv=pltpu.SemaphoreType.DMA((4 * EXPERTS,)),
 )
 

time: 102 us -> 100 us (0.980)
  Pallas kernels: 98.8 us -> 97.2 us
    pallas_call x1, Pallas kernels: 98.8 us -> 97.2 us  [body(): pl.pallas_call(layer_kernel, out_shape=jax.ShapeDtypeStruct((ROWS, HEADS...]
where the time goes in v4:
time: 100 us; the launch traced here: 98.6 us
  Pallas kernels  97.2 us (97%)
  local copies, waits for them, and re-layouts  1.47 us (1%)
    pallas_call x1, Pallas kernels, body(): pl.pallas_call(layer_kernel, out_shape=jax.ShapeDtypeStruct((ROWS, HEADS...  97.2 us

profile of v4, /device:TPU:2, one launch (start us, length us, event | category | flops | bytes accessed | tf_op | source)
XLA Modules:
  0.0 98.6 jit_solution(5602100694657122848)
XLA Ops:
  0.0 97.2 %layer.1 = bf16[64,512]{1,0:T(8,128)(2,1)} custom-call(bf16[64,512]{1,0:T(8,128)(2,1)} %res.1, bf16[64,512]{1,0:T(8,128)(2,1)} %q.1, bf16[1024,128]{1,0:T(8,128)(2,1)} %key.1, bf16[1024,128]{1,0:T(8,128)(2,1)} %value.1, s32[1,64]{1,0:T(1,128)} %bitcast.9, bf16[32,128]{1,0:T(8,128)(2,1)} %bitcast.5, bf16[1,448,4096]{2,1,0:T(8,128)(2,1)} %wg.1, ...), custom_call_target="tpu_custom_call" | custom-call | tf_op jit(solution)/shard_map/layer/pallas_call | solution.py:802
  97.2 1.5 %copy.14 = bf16[64,512]{1,0:T(8,128)(2,1)} copy(bf16[64,512]{1,0:T(8,128)(2,1)} %layer.1) | data formatting | bytes 131072
